TPU v7x, 128 devices: a whole 4x4x4 slice. The times are simulated.
128 devices in a mesh: seq: 32 (over z, y, core), width: 4 (over x).
Axes of the slice: x: 4, y: 4, z: 4, core: 2. Of those that a mesh axis runs over, the one named last changes fastest.
Arguments:
- tokens: bfloat16 [32768, 4096], P('seq', 'width'), may hold values from -8 to 8
- slot_param: bfloat16 [4096, 1024], P('width'), may hold values from -10 to 10
- scale: float32 [1], replicated, may hold values from 250 to 400
- w_in: bfloat16 [8, 4096, 16384], P(None, 'width', 'seq'), may hold values from -0.09375 to 0.09375
- w_out: bfloat16 [8, 16384, 4096], P(None, 'seq', 'width'), may hold values from -0.046875 to 0.046875
Outputs:
- mixed: bfloat16 [32768, 4096], P('seq', 'width')
All inputs are finite; a program needn't handle non-finite values.
Results may differ from a plain program's by a relative error of at most 0.012.
Values may be sent and summed in bfloat16 or wider, within the bound.
A program may use at most 128 MiB of HBM per device.

v0:
```python
import jax
import jax.numpy as jnp
from jax import lax
from jax.sharding import PartitionSpec as P

SLOT_PER = 16
E_RUN = 8
WINDOW = 128


EPS = 1e-06


def per_device(tokens, slot_param, scale, w_in, w_out):
    width_local = tokens.shape[1]
    raw_part = jnp.dot(tokens, slot_param, preferred_element_type=jnp.float32)
    token_float = tokens.astype(jnp.float32)
    row_squares = jnp.sum(token_float * token_float, axis=1)
    param_float = slot_param.astype(jnp.float32)
    column_squares = jnp.sum(param_float * param_float, axis=0)
    raw, row_total, column_total = lax.psum((raw_part, row_squares, column_squares), "width")
    logits = (
        scale[0]
        * raw
        / (jnp.sqrt(row_total + EPS)[:, None] * jnp.sqrt(column_total + EPS)[None, :])
    )
    window_logits = logits[:, :WINDOW]
    token_max = jnp.max(logits, axis=1)
    token_total = jnp.sum(jnp.exp(logits - token_max[:, None]), axis=1)
    slot_max = lax.pmax(jnp.max(window_logits, axis=0), "seq")
    dispatch = jnp.exp(window_logits - slot_max[None, :]).astype(jnp.bfloat16)
    part_total = jnp.sum(dispatch.astype(jnp.float32), axis=0)
    weighted = jnp.einsum("tw,td->wd", dispatch, tokens, preferred_element_type=jnp.float32)
    weighted_all, slot_total = lax.psum((weighted, part_total), "seq")
    slot_in = (weighted_all / slot_total[:, None]).astype(jnp.bfloat16)
    grouped = slot_in.reshape(E_RUN, SLOT_PER, width_local)
    hidden_part = jnp.einsum("epd,edf->epf", grouped, w_in, preferred_element_type=jnp.float32)
    hidden_sum = lax.psum(hidden_part, "width")
    hidden = jax.nn.gelu(hidden_sum, approximate=False).astype(jnp.bfloat16)
    output_part = jnp.einsum("epf,efd->epd", hidden, w_out, preferred_element_type=jnp.float32)
    output_part = output_part.reshape(WINDOW, width_local)
    slot_out = lax.psum(output_part, "seq").astype(jnp.bfloat16)
    combine = (jnp.exp(window_logits - token_max[:, None]) / token_total[:, None]).astype(
        jnp.bfloat16
    )
    return jnp.dot(combine, slot_out, preferred_element_type=jnp.float32).astype(jnp.bfloat16)


def solution(mesh):
    in_specs = (
        P("seq", "width"),
        P("width", None),
        P(),
        P(None, "width", "seq"),
        P(None, "seq", "width"),
    )
    out_specs = P("seq", "width")
    return jax.shard_map(
        per_device, mesh=mesh, in_specs=in_specs, out_specs=out_specs, check_vma=False
    )
```

profile of v0, /device:TPU:1, one launch (start us, length us, event | category | flops | bytes accessed | tf_op | source)
XLA Modules:
  0.0 471.0 jit_solution(4180506795895283633)
XLA Ops:
  6.5 0.0 all-reduce.6.cloned.1.call-start
  6.5 6.5 %fusion.77 = f32[1024,1024]{1,0:T(8,128)} fusion(bf16[1024,1024]{1,0:T(8,128)(2,1)} %param.5, bf16[1024,1024]{1,0:T(8,128)(2,1)} %param.6), kind=kOutput, calls=%fused_computation.97 | convolution fusion | flops 2147483648 | bytes 8388608 | tf_op jit(solution)/shard_map/dot_general | solution.py:16
  13.1 0.0 copy-start.1
  13.1 0.0 all-reduce.6.cloned.1.call-update
  13.1 0.0 all-reduce.8.cloned.1.call-start
  13.9 2.1 multiply_reduce_fusion
  16.0 0.0 copy-done.1
  16.0 0.5 multiply_reduce_fusion.1
  16.5 9.4 %all-reduce = (f32[1024]{0:T(1024)S(1)}, f32[1024]{0:T(1024)S(1)}) all-reduce(f32[1024]{0:T(1024)S(1)} %multiply_reduce_fusion, f32[1024]{0:T(1024)S(1)} %multiply_reduce_fusion.1), channel_id=1, replica_groups=mesh['seq'=32,'width'=4] {'width'}, use_global_device_ids=true, to_apply=%region_4.0 | all-reduce | flops 2048 | bytes 16384 | tf_op jit(solution)/shard_map/psum | solution.py:21
  25.9 83.3 %all-reduce.6.cloned.1.call-done = f32[1024,1024]{1,0:T(8,128)} async-done(((f32[1024,1024]{1,0:T(8,128)}), f32[1024,1024]{1,0:T(8,128)}) %all-reduce.6.cloned.1.call-update) | async-done | bytes 4194320 | tf_op jit(solution)/shard_map/psum | solution.py:21
  109.2 3.4 fusion.76
  112.6 0.0 copy-start
  112.6 1.9 copy-done
  114.5 0.1 slice_reduce_fusion
  114.7 62.9 %pmax.7 = f32[128]{0:T(128)S(1)} all-reduce(f32[128]{0:T(128)S(1)} %slice_reduce_fusion), channel_id=1, replica_groups=mesh['seq'=32,'width'=4] {'seq'}, use_global_device_ids=true, to_apply=%region_8.0 | all-reduce | flops 128 | bytes 1024 | tf_op jit(solution)/shard_map/pmax | solution.py:30
  177.5 2.3 fusion.45
  179.9 0.0 all-reduce.8.cloned.1.call-update
  179.9 0.0 all-reduce.10.cloned.1.call-start
  179.9 1.2 convert_reduce_fusion
  181.1 67.1 %psum.53 = f32[128]{0:T(128)S(1)} all-reduce(f32[128]{0:T(128)S(1)} %convert_reduce_fusion), channel_id=1, replica_groups=mesh['seq'=32,'width'=4] {'seq'}, use_global_device_ids=true, to_apply=%region_11.0 | all-reduce | flops 128 | bytes 1024 | tf_op jit(solution)/shard_map/psum | solution.py:34
  248.2 34.9 %all-reduce.8.cloned.1.call-done = f32[128,1024]{1,0:T(8,128)} async-done(((f32[128,1024]{1,0:T(8,128)}), f32[128,1024]{1,0:T(8,128)}) %all-reduce.8.cloned.1.call-update) | async-done | bytes 524304 | tf_op jit(solution)/shard_map/psum | solution.py:34
  283.1 1.1 divide_convert_fusion
  284.2 5.3 %fusion.78 = f32[8,16,512]{2,1,0:T(8,128)} fusion(bf16[8,16,1024]{2,1,0:T(8,128)(2,1)S(1)} %bitcast.11, bf16[8,1024,512]{2,1,0:T(8,128)(2,1)} %param.8), kind=kOutput, calls=%fused_computation.98 | convolution fusion | flops 134217728 | bytes 8912896 | tf_op jit(solution)/shard_map/epd,edf->epf/dot_general | solution.py:37
  289.5 0.0 all-reduce.10.cloned.1.call-update
  289.5 3.1 exponential_reduce_fusion
  292.6 36.0 %all-reduce.10.cloned.1.call-done = f32[8,16,512]{2,1,0:T(8,128)} async-done(((f32[8,16,512]{2,1,0:T(8,128)}), f32[8,16,512]{2,1,0:T(8,128)}) %all-reduce.10.cloned.1.call-update) | async-done | bytes 262160 | tf_op jit(solution)/shard_map/psum | solution.py:38
  328.6 5.1 %fusion.13 = f32[8,16,1024]{2,1,0:T(8,128)S(1)} fusion(bf16[8,512,1024]{2,1,0:T(8,128)(2,1)} %param.9, f32[8,16,512]{2,1,0:T(8,128)} %all-reduce.10.cloned.1.call-done), kind=kOutput, calls=%fused_computation.32 | convolution fusion | flops 138477568 | bytes 9175040 | tf_op jit(solution)/shard_map/epf,efd->epd/dot_general | solution.py:40
  333.7 127.7 %all-reduce.11 = bf16[128,1024]{1,0:T(8,128)(2,1)S(1)} all-reduce(f32[128,1024]{1,0:T(8,128)S(1)} %bitcast.12), channel_id=1, replica_groups=mesh['seq'=32,'width'=4] {'seq'}, use_global_device_ids=true, to_apply=%region_13.0 | all-reduce | flops 131072 | bytes 786432 | tf_op jit(solution)/shard_map/psum | solution.py:42
  461.4 3.1 convolution_convert_fusion
  (1 shorter events, 0.0 us)
Async XLA Ops:
  6.5 102.6 %all-reduce.6.cloned.1.call-start = ((), (), s32[]{:S(2)}) async-start(), calls=%async_computation | async-start | bytes 8388608 | tf_op jit(solution)/shard_map/psum | solution.py:21
  13.1 2.9 copy-start.1
  13.1 270.0 %all-reduce.8.cloned.1.call-start = ((), (), s32[]{:S(2)}) async-start(), calls=%async_computation.1 | async-start | bytes 1048576 | tf_op jit(solution)/shard_map/psum | solution.py:34
  112.6 1.9 copy-start
  179.9 148.8 %all-reduce.10.cloned.1.call-start = ((), (), s32[]{:S(2)}) async-start(), calls=%async_computation.2 | async-start | bytes 524288 | tf_op jit(solution)/shard_map/psum | solution.py:38
Sparse Core Ops, SparseCore 0:
  13.2 95.9 all-reduce.5
  180.0 103.0 all-reduce.7
  289.7 38.9 all-reduce.9
where the time goes:
time: 476 us; the launch traced here: 471 us
  blocking collectives  267 us (56%)
  waiting for transfers between devices  154 us (32%)
  matrix products  22.3 us (5%)
  between operations  13.9 us (3%)
  other arithmetic  11.5 us (2%)
    psum x1, blocking collectives, per_device(): slot_out = lax.psum(output_part, 'seq').astype(jnp.bfloat16)  128 us
    psum x1, waiting for transfers between devices, per_device(): lax.psum((raw_part, row_squares, column_squares), 'width')  83.3 us
    psum x1, blocking collectives, per_device(): weighted_all, slot_total = lax.psum((weighted, part_total), 'seq')  67.1 us
    pmax x1, blocking collectives, per_device(): slot_max = lax.pmax(jnp.max(window_logits, axis=0), 'seq')  62.9 us
    psum x1, waiting for transfers between devices, per_device(): hidden_sum = lax.psum(hidden_part, 'width')  36 us
    psum x1, waiting for transfers between devices, per_device(): weighted_all, slot_total = lax.psum((weighted, part_total), 'seq')  34.9 us
  transfers between devices with their start and end apart: 3, of which 3 were waited for; matrix products, arithmetic and copies ran while one was open for 1% of the time, Pallas kernels for 0%

commit v1 on v0

v1 whole, which is shorter than its diff:
```python
import jax
import jax.numpy as jnp
from jax import lax
from jax.experimental import pallas as pl
from jax.experimental.pallas import tpu as pltpu
from jax.sharding import PartitionSpec as P

SLOT_PER = 16
E_RUN = 8
WINDOW = 128
EPS = 1e-06
F32 = jnp.float32
BF16 = jnp.bfloat16
MESH = pl.DeviceIdType.MESH
QT = 256
REST = 896
CHIPS = 16
SENDS = (2, 1, 3)
ARRIVALS = (0, 1, 3, 2)


def column(row):
    return jnp.transpose(jnp.broadcast_to(row, (128, 128)))


def kernel(
    tok_h, sp_h, scale_ref, win_h, wout_h,
    comb_o, so_o,
    tok, spw, spn, win, wout,
    wsend, wrecv, lw, rnv, dsp, nsend, nrecv,
    wb, pr, ab, rb, gs, si,
    hp, hr, hb, ob, po, ab2, ro, so, cb,
    ld_sem, x_send, x_recv, c_send, c_recv, s_send, s_recv, f_send, f_recv,
):
    s = lax.axis_index("seq")
    x = lax.axis_index("width")
    c = lax.rem(s, 2)
    p = lax.div(s, 2)
    z = lax.div(p, 4)
    y = lax.rem(p, 4)
    peer = (s + 1 - 2 * c, x)

    def xdev(d):
        return (s, lax.rem(x + d, 4))

    def chip_of(j):
        return lax.rem(z + j // 4, 4) * 4 + lax.rem(y + j % 4, 4)

    def chip_from(j):
        return lax.rem(z + 4 - j // 4, 4) * 4 + lax.rem(y + 4 - j % 4, 4)

    pending = []

    def remote(src, dst, send, recv, to):
        cp = pltpu.make_async_remote_copy(
            src_ref=src, dst_ref=dst, send_sem=send, recv_sem=recv, device_id=to, device_id_type=MESH
        )
        cp.start()
        pending.append(cp)
        return cp

    def load(src, dst, i):
        cp = pltpu.make_async_copy(src, dst, ld_sem.at[i])
        cp.start()
        return cp

    ld_spw = load(sp_h.at[:, pl.ds(0, WINDOW)], spw, 0)
    ld_tok = {}
    for i, d in enumerate((2, 1, 3, 0)):
        rows = pl.ds(lax.rem(x + d, 4) * QT, QT)
        ld_tok[d] = load(tok_h.at[rows], tok.at[rows], 1 + i)
    ld_spn = load(sp_h.at[:, pl.ds(WINDOW, REST)], spn, 5)
    ld_win = {}
    for i, d in enumerate((2, 1, 3, 0)):
        e = 2 * lax.rem(x + d, 4)
        ld_win[d] = load(win_h.at[pl.ds(e, 2)], win.at[pl.ds(e, 2)], 6 + i)
    ld_wout = {}
    for i, d in enumerate(ARRIVALS):
        e = 2 * lax.rem(x + 4 - d, 4)
        ld_wout[d] = load(wout_h.at[pl.ds(e, 2)], wout.at[pl.ds(e, 2)], 10 + i)

    barrier = pltpu.get_barrier_semaphore()
    for d in (1, 2, 3):
        pl.semaphore_signal(barrier, inc=1, device_id=xdev(d), device_id_type=MESH)
    pl.semaphore_signal(barrier, inc=1, device_id=peer, device_id_type=MESH)
    for j in range(1, CHIPS):
        pl.semaphore_signal(barrier, inc=1, device_id=(chip_of(j) * 2 + c, x), device_id_type=MESH)

    ld_spw.wait()
    spf = spw[...].astype(F32)
    csq = jnp.sum(spf * spf, axis=0, keepdims=True)
    xw = {}
    for d in (2, 1, 3, 0):
        ld_tok[d].wait()
        t = tok[pl.ds(lax.rem(x + d, 4) * QT, QT), :]
        wsend[d, 0:QT, :] = jnp.dot(t, spw[...], preferred_element_type=F32)
        part = jnp.zeros((QT, 128), F32)
        for b in range(8):
            tf = t[:, b * 128:(b + 1) * 128].astype(F32)
            part = part + tf * tf
        rows = [jnp.sum(jnp.transpose(part[h * 128:(h + 1) * 128]), axis=0, keepdims=True) for h in range(2)]
        wsend[d, QT:QT + 8, :] = jnp.concatenate(rows + [csq, jnp.zeros((5, 128), F32)], axis=0)
        if d == 2:
            pl.semaphore_wait(barrier, 19)
        if d:
            xw[d] = remote(wsend.at[d], wrecv.at[d], x_send.at[0, d], x_recv.at[0, d], xdev(d))
    tot = wsend[0]
    for d in (1, 3, 2):
        xw[d].wait_recv()
        tot = tot + wrecv[d]
    rn = jnp.sqrt(jnp.concatenate([column(tot[QT:QT + 1]), column(tot[QT + 1:QT + 2])], axis=0) + EPS)
    cn = jnp.sqrt(tot[QT + 2:QT + 3] + EPS)
    scale = scale_ref[0]
    logits = scale * tot[0:QT] / (rn * cn)
    lw[...] = logits
    rnv[...] = rn
    m = jnp.max(logits, axis=0, keepdims=True).astype(BF16)
    dsp[x, 0:QT, :] = jnp.exp(logits - m.astype(F32)).astype(BF16)
    dsp[x, QT:QT + 16, :] = jnp.broadcast_to(m, (16, 128))
    xd = {d: remote(dsp.at[x], dsp.at[x], x_send.at[1, d], x_recv.at[1, d], xdev(d)) for d in SENDS}

    ld_spn.wait()
    csn = jnp.zeros((8, REST), F32)
    for b in range(32):
        sf = spn[b * 32:(b + 1) * 32, :].astype(F32)
        sq = sf * sf
        csn = csn + sq[0:8] + sq[8:16] + sq[16:24] + sq[24:32]
    xn = {}
    for d in (2, 1, 3, 0):
        t = tok[pl.ds(lax.rem(x + d, 4) * QT, QT), :]
        nsend[d, 0:QT, :] = jnp.dot(t, spn[...], preferred_element_type=F32)
        nsend[d, QT:QT + 8, :] = csn
        if d:
            xn[d] = remote(nsend.at[d], nrecv.at[d], x_send.at[2, d], x_recv.at[2, d], xdev(d))

    for d in SENDS:
        xd[d].wait_recv()
    ms = [dsp[q, QT:QT + 1, :].astype(F32) for q in range(4)]
    mseq = jnp.maximum(jnp.maximum(ms[0], ms[1]), jnp.maximum(ms[2], ms[3]))
    total = jnp.zeros((1, 128), F32)
    cols = []
    for q in range(4):
        f = jnp.exp(ms[q] - mseq)
        total = total + f * jnp.sum(dsp[q, 0:QT, :].astype(F32), axis=0, keepdims=True)
        cols.append(column(f))
    stats = jnp.concatenate([mseq, total, jnp.zeros((6, 128), F32)], axis=0)
    for h in range(2):
        for k in range(2):
            at = h * 512 + k * 256
            acc = jnp.zeros((128, 256), F32)
            for q in range(4):
                prod = lax.dot_general(
                    dsp[q, 0:QT, :], tok[q * QT:(q + 1) * QT, at:at + 256],
                    (((0,), (0,)), ((), ())), preferred_element_type=F32,
                )
                acc = acc + prod * jnp.concatenate([cols[q], cols[q]], axis=1)
            for e in range(E_RUN):
                for b in range(2):
                    wb[k, e * 2 + h, b * 16:(b + 1) * 16, :] = acc[e * 16:(e + 1) * 16, b * 128:(b + 1) * 128]
                wb[k, e * 2 + h, 32:40, :] = stats

    cw = remote(wb.at[1 - c], pr, c_send.at[0], c_recv.at[0], peer)
    cw.wait_recv()
    m_a, m_b = wb[c, 0, 32:33, :], pr[0, 32:33, :]
    m2 = jnp.maximum(m_a, m_b)
    f_a, f_b = jnp.exp(m_a - m2), jnp.exp(m_b - m2)
    t2 = f_a * wb[c, 0, 33:34, :] + f_b * pr[0, 33:34, :]
    stats = jnp.concatenate([m2, t2, jnp.zeros((6, 128), F32)], axis=0)
    c_a, c_b = column(f_a), column(f_b)
    for i in range(CHIPS):
        e = i // 2
        k_a, k_b = c_a[e * 16:(e + 1) * 16], c_b[e * 16:(e + 1) * 16]
        for b in range(2):
            r = slice(b * 16, (b + 1) * 16)
            ab[i, r, :] = wb[c, i, r, :] * k_a + pr[i, r, :] * k_b
        ab[i, 32:40, :] = stats
    sw = {
        j: remote(ab.at[chip_of(j)], rb.at[j], s_send.at[0, j], s_recv.at[0, j], (chip_of(j) * 2 + c, x))
        for j in range(1, CHIPS)
    }
    for j in range(1, CHIPS):
        sw[j].wait_recv()
    mr = [ab[p, 32:33, :]] + [rb[j, 32:33, :] for j in range(1, CHIPS)]
    tr = [ab[p, 33:34, :]] + [rb[j, 33:34, :] for j in range(1, CHIPS)]
    top = mr[0]
    for v in mr[1:]:
        top = jnp.maximum(top, v)
    fr = [jnp.exp(v - top) for v in mr]
    total = fr[0] * tr[0]
    for f, t in zip(fr[1:], tr[1:]):
        total = total + f * t
    gs[...] = jnp.transpose(jnp.concatenate([f / total for f in fr] + [jnp.zeros((112, 128), F32)], axis=0))
    ge = gs[pl.ds(lax.div(p, 2) * 16, 16), :]
    acc = [jnp.zeros((16, 128), F32)] * 2
    for j in range(CHIPS):
        w = ge[:, j:j + 1]
        for b in range(2):
            r = slice(b * 16, (b + 1) * 16)
            v = ab[p, r, :] if j == 0 else rb[j, r, :]
            acc[b] = acc[b] + v * w
    si[p, c, :, :] = jnp.concatenate(acc, axis=0).astype(BF16)

    def gather(buf, k):
        own = remote(buf.at[p, c], buf.at[p, c], f_send.at[k, 0], f_recv.at[k, 0], peer)
        out = {
            j: remote(buf.at[p, c], buf.at[p, c], s_send.at[k, j], s_recv.at[k, j], (chip_of(j) * 2 + c, x))
            for j in range(1, CHIPS)
        }
        fwd = [own]
        for j in range(1, CHIPS):
            out[j].wait_recv()
            at = chip_from(j)
            fwd.append(remote(buf.at[at, c], buf.at[at, c], f_send.at[k, j], f_recv.at[k, j], peer))
        for cp in fwd:
            cp.wait_recv()

    gather(si, 1)

    xh = {}
    for d in (2, 1, 3, 0):
        q = lax.rem(x + d, 4)
        ld_win[d].wait()
        for k in range(2):
            e = 2 * q + k
            rows = jnp.concatenate(
                [si[e * 2 + h, g, b * 16:(b + 1) * 16, :] for h in range(2) for g in range(2) for b in range(2)],
                axis=1,
            )
            hp[d, k * 16:(k + 1) * 16, :] = jnp.dot(rows, win[e], preferred_element_type=F32)
        if d:
            xh[d] = remote(hp.at[d], hr.at[d], x_send.at[3, d], x_recv.at[3, d], xdev(d))
    hidden = hp[0]
    for d in (1, 3, 2):
        xh[d].wait_recv()
        hidden = hidden + hr[d]
    hidden = 0.5 * hidden * (1.0 + lax.erf(hidden * 0.7071067811865476))
    hb[x] = hidden.astype(BF16)
    xg = {d: remote(hb.at[x], hb.at[x], x_send.at[4, d], x_recv.at[4, d], xdev(d)) for d in SENDS}

    for d in ARRIVALS:
        q = lax.rem(x + 4 - d, 4)
        if d:
            xg[d].wait_recv()
        ld_wout[d].wait()
        for k in range(2):
            e = 2 * q + k
            o = jnp.dot(hb[q, k * 16:(k + 1) * 16, :], wout[e], preferred_element_type=F32)
            for h in range(2):
                for g in range(2):
                    for b in range(2):
                        at = h * 512 + g * 256 + b * 128
                        ob[g, e * 2 + h, b * 16:(b + 1) * 16, :] = o[:, at:at + 128]
    co = remote(ob.at[1 - c], po, c_send.at[1], c_recv.at[1], peer)
    co.wait_recv()
    ab2[...] = ob[c] + po[...]
    sv = {
        j: remote(ab2.at[chip_of(j)], ro.at[j], s_send.at[2, j], s_recv.at[2, j], (chip_of(j) * 2 + c, x))
        for j in range(1, CHIPS)
    }

    for d in (1, 3, 2):
        xn[d].wait_recv()
    cs = nsend[0, QT:QT + 8, :] + nrecv[1, QT:QT + 8, :] + nrecv[2, QT:QT + 8, :] + nrecv[3, QT:QT + 8, :]
    cnn = jnp.sqrt(jnp.sum(cs, axis=0, keepdims=True) + EPS)
    for g in range(4):
        r = slice(g * 64, (g + 1) * 64)
        rg = rnv[r, :]
        lwin = lw[r, :]
        ls = []
        top = lwin
        for b in range(7):
            at = slice(b * 128, (b + 1) * 128)
            raw = nsend[0, r, at] + nrecv[1, r, at] + nrecv[2, r, at] + nrecv[3, r, at]
            lg = scale * raw / (rg * cnn[:, at])
            ls.append(lg)
            top = jnp.maximum(top, lg)
        tmax = jnp.max(top, axis=1, keepdims=True)
        ew = jnp.exp(lwin - tmax)
        tsum = ew
        for lg in ls:
            tsum = tsum + jnp.exp(lg - tmax)
        ttot = jnp.sum(tsum, axis=1, keepdims=True)
        cb[x, r, :] = (ew / ttot).astype(BF16)
    xc = {d: remote(cb.at[x], cb.at[x], x_send.at[5, d], x_recv.at[5, d], xdev(d)) for d in SENDS}

    for j in range(1, CHIPS):
        sv[j].wait_recv()
    acc = ab2[p]
    for j in range(1, CHIPS):
        acc = acc + ro[j]
    so[p, c, :, :] = acc.astype(BF16)
    gather(so, 3)
    for d in SENDS:
        xc[d].wait_recv()
    for q in range(4):
        comb_o[q * QT:(q + 1) * QT, :] = cb[q]
    for e in range(E_RUN):
        for h in range(2):
            for g in range(2):
                for b in range(2):
                    at = h * 512 + g * 256 + b * 128
                    so_o[e * 16:(e + 1) * 16, at:at + 128] = so[e * 2 + h, g, b * 16:(b + 1) * 16, :]
    for cp in pending:
        cp.wait_send()


def per_device(tokens, slot_param, scale, w_in, w_out):
    vm = pltpu.VMEM
    dma = pltpu.SemaphoreType.DMA
    anyspec = pl.BlockSpec(memory_space=pl.ANY)
    vspec = pl.BlockSpec(memory_space=pltpu.VMEM)
    comb, slot_out = pl.pallas_call(
        kernel,
        name="moe_exchange",
        out_shape=(jax.ShapeDtypeStruct((1024, 128), BF16), jax.ShapeDtypeStruct((128, 1024), BF16)),
        in_specs=[anyspec, anyspec, pl.BlockSpec(memory_space=pltpu.SMEM), anyspec, anyspec],
        out_specs=(vspec, vspec),
        scratch_shapes=[
            vm((1024, 1024), BF16), vm((1024, 128), BF16), vm((1024, REST), BF16),
            vm((8, 1024, 512), BF16), vm((8, 512, 1024), BF16),
            vm((4, QT + 8, 128), F32), vm((4, QT + 8, 128), F32), vm((QT, 128), F32), vm((QT, 128), F32),
            vm((4, QT + 16, 128), BF16),
            vm((4, QT + 8, REST), F32), vm((4, QT + 8, REST), F32),
            vm((2, 16, 40, 128), F32), vm((16, 40, 128), F32), vm((16, 40, 128), F32), vm((16, 40, 128), F32),
            vm((128, 128), F32), vm((16, 2, 32, 128), BF16),
            vm((4, 32, 512), F32), vm((4, 32, 512), F32), vm((4, 32, 512), BF16),
            vm((2, 16, 32, 128), F32), vm((16, 32, 128), F32), vm((16, 32, 128), F32), vm((16, 32, 128), F32),
            vm((16, 2, 32, 128), BF16), vm((4, QT, 128), BF16),
            dma((14,)), dma((6, 4)), dma((6, 4)), dma((2,)), dma((2,)),
            dma((4, 16)), dma((4, 16)), dma((4, 16)), dma((4, 16)),
        ],
        compiler_params=pltpu.CompilerParams(
            collective_id=0, has_side_effects=True, vmem_limit_bytes=56 * 2**20
        ),
    )(tokens, slot_param, scale, w_in, w_out)
    return jnp.dot(comb, slot_out, preferred_element_type=F32).astype(BF16)


def solution(mesh):
    in_specs = (
        P("seq", "width"),
        P("width", None),
        P(),
        P(None, "width", "seq"),
        P(None, "seq", "width"),
    )
    return jax.shard_map(
        per_device, mesh=mesh, in_specs=in_specs, out_specs=P("seq", "width"), check_vma=False
    )
```

time: 476 us -> 92.7 us (0.19); the launches traced: 471 us -> 92.6 us
  blocking collectives: 267 us -> 0 us
  waiting for transfers between devices: 154 us -> 0 us
  Pallas kernels: 0 us -> 88.9 us
  matrix products: 22.3 us -> 3.04 us
  between operations: 13.9 us -> 0.66 us
  other arithmetic: 11.5 us -> 0 us
    psum x3 -> x0, blocking collectives: 204 us -> none  [the longest x1 128 us: per_device(): slot_out = lax.psum(output_part, 'seq').astype(jnp.bfloat16)]
    psum x3 -> x0, waiting for transfers between devices: 154 us -> none  [the longest x1 83.3 us: per_device(): lax.psum((raw_part, row_squares, column_squares), 'width')]
    pallas_call x0 -> x1, Pallas kernels: none -> 88.9 us  [per_device(): pl.pallas_call(kernel, name='moe_exchange', out_shape=(jax.ShapeDtypeStru...]
    pmax x1 -> x0, blocking collectives: 62.9 us -> none  [per_device(): slot_max = lax.pmax(jnp.max(window_logits, axis=0), 'seq')]
    dot_general x5 -> x1, matrix products: 22.3 us -> 3.04 us  [per_device(): return jnp.dot(comb, slot_out, preferred_element_type=F32).astype(BF16)]
    reduce_sum x4 -> x0, other arithmetic: 6.83 us -> none  [the longest x1 3.09 us: per_device(): token_total = jnp.sum(jnp.exp(logits - token_max[:, None]), axis=1)]
  transfers between devices with their start and end apart: 3 -> 0, of which waited for: 3 -> 0; matrix products, arithmetic and copies ran while one was open for 1% -> 0% of each run, Pallas kernels for 0% -> 0%
where the time goes in v1:
time: 92.7 us; the launch traced here: 92.6 us
  Pallas kernels  88.9 us (96%)
  matrix products  3.04 us (3%)
    pallas_call x1, Pallas kernels, per_device(): pl.pallas_call(kernel, name='moe_exchange', out_shape=(jax.ShapeDtypeStru...  88.9 us
    dot_general x1, matrix products, per_device(): return jnp.dot(comb, slot_out, preferred_element_type=F32).astype(BF16)  3.04 us

profile of v1, /device:TPU:1, one launch (start us, length us, event | category | flops | bytes accessed | tf_op | source)
XLA Modules:
  0.0 92.6 jit_solution(5482907428466940052)
XLA Ops:
  0.7 88.9 %moe_exchange.1 = (bf16[1024,128]{1,0:T(8,128)(2,1)}, bf16[128,1024]{1,0:T(8,128)(2,1)}) custom-call(bf16[1024,1024]{1,0:T(8,128)(2,1)} %tok_h.1, bf16[1024,1024]{1,0:T(8,128)(2,1)} %sp_h.1, f32[1]{0:T(128)S(6)} %copy.6.scale_ref, bf16[8,1024,512]{2,1,0:T(8,128)(2,1)} %win_h.1, bf16[8,512,1024]{2,1,0:T(8,128)(2,1)} %wout_h.1), custom_call_target="tpu_custom_call" | custom-call | tf_op jit(solution)/shard_map/moe_exchange/pallas_call | solution.py:312
  89.6 3.0 %convolution_convert_fusion = bf16[1024,1024]{1,0:T(8,128)(2,1)} fusion(bf16[1024,128]{1,0:T(8,128)(2,1)} %get-tuple-element.7, bf16[128,1024]{1,0:T(8,128)(2,1)} %get-tuple-element.8), kind=kOutput, calls=%fused_computation | convolution fusion | flops 269484032 | bytes 2621440 | tf_op jit(solution)/shard_map/dot_general | solution.py:336

commit v2 on v1

--- a/solution.py
+++ b/solution.py
@@ -17,6 +17,7 @@
 CHIPS = 16
 SENDS = (2, 1, 3)
 ARRIVALS = (0, 1, 3, 2)
+GROUPS = (0, 1, 3, 2)
 
 
 def column(row):
@@ -27,7 +28,7 @@
     tok_h, sp_h, scale_ref, win_h, wout_h,
     comb_o, so_o,
     tok, spw, spn, win, wout,
-    wsend, wrecv, lw, rnv, dsp, nsend, nrecv,
+    wsend, wrecv, lw, rnv, dsp, nsend, nrecv, relay_a, relay_b,
     wb, pr, ab, rb, gs, si,
     hp, hr, hb, ob, po, ab2, ro, so, cb,
     ld_sem, x_send, x_recv, c_send, c_recv, s_send, s_recv, f_send, f_recv,
@@ -56,8 +57,20 @@
             src_ref=src, dst_ref=dst, send_sem=send, recv_sem=recv, device_id=to, device_id_type=MESH
         )
         cp.start()
-        pending.append(cp)
+        pending.append((None, cp))
         return cp
+
+    def remote_if(cond, src, dst, send, recv, to):
+        cp = pltpu.make_async_remote_copy(
+            src_ref=src, dst_ref=dst, send_sem=send, recv_sem=recv, device_id=to, device_id_type=MESH
+        )
+        pl.when(cond)(cp.start)
+        pending.append((cond, cp))
+
+    def arrival(dst, send, recv):
+        return pltpu.make_async_remote_copy(
+            src_ref=dst, dst_ref=dst, send_sem=send, recv_sem=recv, device_id=peer, device_id_type=MESH
+        )
 
     def load(src, dst, i):
         cp = pltpu.make_async_copy(src, dst, ld_sem.at[i])
@@ -70,15 +83,6 @@
         rows = pl.ds(lax.rem(x + d, 4) * QT, QT)
         ld_tok[d] = load(tok_h.at[rows], tok.at[rows], 1 + i)
     ld_spn = load(sp_h.at[:, pl.ds(WINDOW, REST)], spn, 5)
-    ld_win = {}
-    for i, d in enumerate((2, 1, 3, 0)):
-        e = 2 * lax.rem(x + d, 4)
-        ld_win[d] = load(win_h.at[pl.ds(e, 2)], win.at[pl.ds(e, 2)], 6 + i)
-    ld_wout = {}
-    for i, d in enumerate(ARRIVALS):
-        e = 2 * lax.rem(x + 4 - d, 4)
-        ld_wout[d] = load(wout_h.at[pl.ds(e, 2)], wout.at[pl.ds(e, 2)], 10 + i)
-
     barrier = pltpu.get_barrier_semaphore()
     for d in (1, 2, 3):
         pl.semaphore_signal(barrier, inc=1, device_id=xdev(d), device_id_type=MESH)
@@ -104,6 +108,26 @@
             pl.semaphore_wait(barrier, 19)
         if d:
             xw[d] = remote(wsend.at[d], wrecv.at[d], x_send.at[0, d], x_recv.at[0, d], xdev(d))
+    ld_win = {}
+    for i, dz in enumerate(GROUPS):
+        e = 2 * lax.rem(z + 4 - dz, 4)
+        ld_win[dz] = load(win_h.at[pl.ds(e, 2)], win.at[pl.ds(e, 2)], 6 + i)
+    ld_wout = {}
+    for i, d in enumerate(ARRIVALS):
+        e = 2 * lax.rem(x + 4 - d, 4)
+        ld_wout[d] = load(wout_h.at[pl.ds(e, 2)], wout.at[pl.ds(e, 2)], 10 + i)
+
+    ld_spn.wait()
+    csn = jnp.zeros((8, REST), F32)
+    for b in range(32):
+        sf = spn[b * 32:(b + 1) * 32, :].astype(F32)
+        sq = sf * sf
+        csn = csn + sq[0:8] + sq[8:16] + sq[16:24] + sq[24:32]
+    for d in (2, 1, 3, 0):
+        t = tok[pl.ds(lax.rem(x + d, 4) * QT, QT), :]
+        nsend[d, 0:QT, :] = jnp.dot(t, spn[...], preferred_element_type=F32)
+        nsend[d, QT:QT + 8, :] = csn
+
     tot = wsend[0]
     for d in (1, 3, 2):
         xw[d].wait_recv()
@@ -119,22 +143,15 @@
     dsp[x, QT:QT + 16, :] = jnp.broadcast_to(m, (16, 128))
     xd = {d: remote(dsp.at[x], dsp.at[x], x_send.at[1, d], x_recv.at[1, d], xdev(d)) for d in SENDS}
 
-    ld_spn.wait()
-    csn = jnp.zeros((8, REST), F32)
-    for b in range(32):
-        sf = spn[b * 32:(b + 1) * 32, :].astype(F32)
-        sq = sf * sf
-        csn = csn + sq[0:8] + sq[8:16] + sq[16:24] + sq[24:32]
-    xn = {}
-    for d in (2, 1, 3, 0):
-        t = tok[pl.ds(lax.rem(x + d, 4) * QT, QT), :]
-        nsend[d, 0:QT, :] = jnp.dot(t, spn[...], preferred_element_type=F32)
-        nsend[d, QT:QT + 8, :] = csn
-        if d:
-            xn[d] = remote(nsend.at[d], nrecv.at[d], x_send.at[2, d], x_recv.at[2, d], xdev(d))
-
     for d in SENDS:
         xd[d].wait_recv()
+    low, high = pl.ds(0, 128), pl.ds(128, QT + 8 - 128)
+    via_a = remote(nsend.at[2, low], relay_a, x_send.at[2, 0], x_recv.at[2, 0], xdev(1))
+    via_b = remote(nsend.at[2, high], relay_b, x_send.at[2, 1], x_recv.at[2, 1], xdev(3))
+    xn = [
+        remote(nsend.at[1, high], nrecv.at[0, high], x_send.at[2, 2], x_recv.at[2, 2], xdev(1)),
+        remote(nsend.at[3, low], nrecv.at[1, low], x_send.at[2, 3], x_recv.at[2, 3], xdev(3)),
+    ]
     ms = [dsp[q, QT:QT + 1, :].astype(F32) for q in range(4)]
     mseq = jnp.maximum(jnp.maximum(ms[0], ms[1]), jnp.maximum(ms[2], ms[3]))
     total = jnp.zeros((1, 128), F32)
@@ -144,13 +161,14 @@
         total = total + f * jnp.sum(dsp[q, 0:QT, :].astype(F32), axis=0, keepdims=True)
         cols.append(column(f))
     stats = jnp.concatenate([mseq, total, jnp.zeros((6, 128), F32)], axis=0)
-    for h in range(2):
-        for k in range(2):
-            at = h * 512 + k * 256
+    cw = None
+    for k in (1 - c, c):
+        for h in range(2):
+            at = pl.multiple_of(h * 512 + k * 256, 256)
             acc = jnp.zeros((128, 256), F32)
             for q in range(4):
                 prod = lax.dot_general(
-                    dsp[q, 0:QT, :], tok[q * QT:(q + 1) * QT, at:at + 256],
+                    dsp[q, 0:QT, :], tok[q * QT:(q + 1) * QT, pl.ds(at, 256)],
                     (((0,), (0,)), ((), ())), preferred_element_type=F32,
                 )
                 acc = acc + prod * jnp.concatenate([cols[q], cols[q]], axis=1)
@@ -158,8 +176,9 @@
                 for b in range(2):
                     wb[k, e * 2 + h, b * 16:(b + 1) * 16, :] = acc[e * 16:(e + 1) * 16, b * 128:(b + 1) * 128]
                 wb[k, e * 2 + h, 32:40, :] = stats
-
-    cw = remote(wb.at[1 - c], pr, c_send.at[0], c_recv.at[0], peer)
+        if cw is None:
+            cw = remote(wb.at[1 - c], pr, c_send.at[0], c_recv.at[0], peer)
+
     cw.wait_recv()
     m_a, m_b = wb[c, 0, 32:33, :], pr[0, 32:33, :]
     m2 = jnp.maximum(m_a, m_b)
@@ -200,36 +219,52 @@
             acc[b] = acc[b] + v * w
     si[p, c, :, :] = jnp.concatenate(acc, axis=0).astype(BF16)
 
+
     def gather(buf, k):
-        own = remote(buf.at[p, c], buf.at[p, c], f_send.at[k, 0], f_recv.at[k, 0], peer)
+        fwd = {0: remote(buf.at[p, c], buf.at[p, c], f_send.at[k, 0], f_recv.at[k, 0], peer)}
         out = {
             j: remote(buf.at[p, c], buf.at[p, c], s_send.at[k, j], s_recv.at[k, j], (chip_of(j) * 2 + c, x))
             for j in range(1, CHIPS)
         }
-        fwd = [own]
-        for j in range(1, CHIPS):
-            out[j].wait_recv()
-            at = chip_from(j)
-            fwd.append(remote(buf.at[at, c], buf.at[at, c], f_send.at[k, j], f_recv.at[k, j], peer))
-        for cp in fwd:
-            cp.wait_recv()
-
-    gather(si, 1)
-
-    xh = {}
-    for d in (2, 1, 3, 0):
-        q = lax.rem(x + d, 4)
-        ld_win[d].wait()
+
+        def arrive(dz):
+            for j in range(dz * 4, dz * 4 + 4):
+                if j:
+                    out[j].wait_recv()
+                    at = chip_from(j)
+                    fwd[j] = remote(buf.at[at, c], buf.at[at, c], f_send.at[k, j], f_recv.at[k, j], peer)
+
+        def whole(dz):
+            for j in range(dz * 4, dz * 4 + 4):
+                fwd[j].wait_recv()
+
+        return arrive, whole
+
+    arrive, whole = gather(si, 1)
+
+    arrive(GROUPS[0])
+    for i, dz in enumerate(GROUPS):
+        if i < 3:
+            arrive(GROUPS[i + 1])
+        whole(dz)
+        q = lax.rem(z + 4 - dz, 4)
+        d = lax.rem(q + 4 - x, 4)
+        ld_win[dz].wait()
         for k in range(2):
             e = 2 * q + k
             rows = jnp.concatenate(
                 [si[e * 2 + h, g, b * 16:(b + 1) * 16, :] for h in range(2) for g in range(2) for b in range(2)],
                 axis=1,
             )
-            hp[d, k * 16:(k + 1) * 16, :] = jnp.dot(rows, win[e], preferred_element_type=F32)
-        if d:
-            xh[d] = remote(hp.at[d], hr.at[d], x_send.at[3, d], x_recv.at[3, d], xdev(d))
-    hidden = hp[0]
+            hp[dz, k * 16:(k + 1) * 16, :] = jnp.dot(rows, win[e], preferred_element_type=F32)
+        remote_if(d != 0, hp.at[dz], hr.at[d], x_send.at[3, dz], x_recv.at[3, d], (s, q))
+
+        @pl.when(d == 0)
+        def _(dz=dz):
+            hr[0] = hp[dz]
+
+    xh = {d: arrival(hr.at[d], x_send.at[3, 0], x_recv.at[3, d]) for d in (1, 2, 3)}
+    hidden = hr[0]
     for d in (1, 3, 2):
         xh[d].wait_recv()
         hidden = hidden + hr[d]
@@ -237,7 +272,22 @@
     hb[x] = hidden.astype(BF16)
     xg = {d: remote(hb.at[x], hb.at[x], x_send.at[4, d], x_recv.at[4, d], xdev(d)) for d in SENDS}
 
-    for d in ARRIVALS:
+    def chips_sum(q, copy):
+        copy.wait_recv()
+        block = pl.ds(4 * q, 4)
+        ab2[block] = ob[c, block] + po[block]
+        dz = lax.rem(q + 4 - z, 4)
+        for dy in range(4):
+            to = q * 4 + lax.rem(y + dy, 4)
+            j = dz * 4 + dy
+            args = (ab2.at[to], ro.at[j], s_send.at[2, j], s_recv.at[2, j], (to * 2 + c, x))
+            if dy:
+                remote(*args)
+            else:
+                remote_if(dz != 0, *args)
+
+    last = None
+    for i, d in enumerate(ARRIVALS):
         q = lax.rem(x + 4 - d, 4)
         if d:
             xg[d].wait_recv()
@@ -250,17 +300,23 @@
                     for b in range(2):
                         at = h * 512 + g * 256 + b * 128
                         ob[g, e * 2 + h, b * 16:(b + 1) * 16, :] = o[:, at:at + 128]
-    co = remote(ob.at[1 - c], po, c_send.at[1], c_recv.at[1], peer)
-    co.wait_recv()
-    ab2[...] = ob[c] + po[...]
-    sv = {
-        j: remote(ab2.at[chip_of(j)], ro.at[j], s_send.at[2, j], s_recv.at[2, j], (chip_of(j) * 2 + c, x))
-        for j in range(1, CHIPS)
-    }
-
-    for d in (1, 3, 2):
-        xn[d].wait_recv()
-    cs = nsend[0, QT:QT + 8, :] + nrecv[1, QT:QT + 8, :] + nrecv[2, QT:QT + 8, :] + nrecv[3, QT:QT + 8, :]
+        block = pl.ds(4 * q, 4)
+        copy = remote(ob.at[1 - c, block], po.at[block], c_send.at[1 + i], c_recv.at[1 + i], peer)
+        if last is not None:
+            chips_sum(*last)
+        last = (q, copy)
+        if d == 0:
+            via_a.wait_recv()
+            nsend[1, low, :] = nsend[1, low, :] + relay_a[...]
+            xn.append(remote(nsend.at[1, low], nrecv.at[0, low], x_send.at[6, 0], x_recv.at[6, 0], xdev(1)))
+            via_b.wait_recv()
+            nsend[3, high, :] = nsend[3, high, :] + relay_b[...]
+            xn.append(remote(nsend.at[3, high], nrecv.at[1, high], x_send.at[6, 1], x_recv.at[6, 1], xdev(3)))
+    chips_sum(*last)
+    sv = {j: arrival(ro.at[j], s_send.at[2, 0], s_recv.at[2, j]) for j in range(1, CHIPS)}
+    for cp in xn:
+        cp.wait_recv()
+    cs = nsend[0, QT:QT + 8, :] + nrecv[0, QT:QT + 8, :] + nrecv[1, QT:QT + 8, :]
     cnn = jnp.sqrt(jnp.sum(cs, axis=0, keepdims=True) + EPS)
     for g in range(4):
         r = slice(g * 64, (g + 1) * 64)
@@ -270,7 +326,7 @@
         top = lwin
         for b in range(7):
             at = slice(b * 128, (b + 1) * 128)
-            raw = nsend[0, r, at] + nrecv[1, r, at] + nrecv[2, r, at] + nrecv[3, r, at]
+            raw = nsend[0, r, at] + nrecv[0, r, at] + nrecv[1, r, at]
             lg = scale * raw / (rg * cnn[:, at])
             ls.append(lg)
             top = jnp.maximum(top, lg)
@@ -289,7 +345,11 @@
     for j in range(1, CHIPS):
         acc = acc + ro[j]
     so[p, c, :, :] = acc.astype(BF16)
-    gather(so, 3)
+    arrive, whole = gather(so, 3)
+    for dz in GROUPS:
+        arrive(dz)
+    for dz in GROUPS:
+        whole(dz)
     for d in SENDS:
         xc[d].wait_recv()
     for q in range(4):
@@ -300,8 +360,11 @@
                 for b in range(2):
                     at = h * 512 + g * 256 + b * 128
                     so_o[e * 16:(e + 1) * 16, at:at + 128] = so[e * 2 + h, g, b * 16:(b + 1) * 16, :]
-    for cp in pending:
-        cp.wait_send()
+    for cond, cp in pending:
+        if cond is None:
+            cp.wait_send()
+        else:
+            pl.when(cond)(cp.wait_send)
 
 
 def per_device(tokens, slot_param, scale, w_in, w_out):
@@ -320,13 +383,13 @@
             vm((8, 1024, 512), BF16), vm((8, 512, 1024), BF16),
             vm((4, QT + 8, 128), F32), vm((4, QT + 8, 128), F32), vm((QT, 128), F32), vm((QT, 128), F32),
             vm((4, QT + 16, 128), BF16),
-            vm((4, QT + 8, REST), F32), vm((4, QT + 8, REST), F32),
+            vm((4, QT + 8, REST), F32), vm((2, QT + 8, REST), F32), vm((128, REST), F32), vm((QT - 120, REST), F32),
             vm((2, 16, 40, 128), F32), vm((16, 40, 128), F32), vm((16, 40, 128), F32), vm((16, 40, 128), F32),
             vm((128, 128), F32), vm((16, 2, 32, 128), BF16),
             vm((4, 32, 512), F32), vm((4, 32, 512), F32), vm((4, 32, 512), BF16),
             vm((2, 16, 32, 128), F32), vm((16, 32, 128), F32), vm((16, 32, 128), F32), vm((16, 32, 128), F32),
             vm((16, 2, 32, 128), BF16), vm((4, QT, 128), BF16),
-            dma((14,)), dma((6, 4)), dma((6, 4)), dma((2,)), dma((2,)),
+            dma((14,)), dma((7, 4)), dma((7, 4)), dma((5,)), dma((5,)),
             dma((4, 16)), dma((4, 16)), dma((4, 16)), dma((4, 16)),
         ],
         compiler_params=pltpu.CompilerParams(

time: 92.7 us -> 75.3 us (0.81)
  Pallas kernels: 88.9 us -> 71.5 us
    pallas_call x1, Pallas kernels: 88.9 us -> 71.5 us  [per_device(): pl.pallas_call(kernel, name='moe_exchange', out_shape=(jax.ShapeDtypeStru...]
where the time goes in v2:
time: 75.3 us; the launch traced here: 75.2 us
  Pallas kernels  71.5 us (95%)
  matrix products  3.04 us (4%)
    pallas_call x1, Pallas kernels, per_device(): pl.pallas_call(kernel, name='moe_exchange', out_shape=(jax.ShapeDtypeStru...  71.5 us
    dot_general x1, matrix products, per_device(): return jnp.dot(comb, slot_out, preferred_element_type=F32).astype(BF16)  3.04 us

profile of v2, /device:TPU:1, one launch (start us, length us, event | category | flops | bytes accessed | tf_op | source)
XLA Modules:
  0.0 75.2 jit_solution(14371580864579789597)
XLA Ops:
  0.7 71.5 %moe_exchange.1 = (bf16[1024,128]{1,0:T(8,128)(2,1)}, bf16[128,1024]{1,0:T(8,128)(2,1)}) custom-call(bf16[1024,1024]{1,0:T(8,128)(2,1)} %tok_h.1, bf16[1024,1024]{1,0:T(8,128)(2,1)} %sp_h.1, f32[1]{0:T(128)S(6)} %copy.6.scale_ref, bf16[8,1024,512]{2,1,0:T(8,128)(2,1)} %win_h.1, bf16[8,512,1024]{2,1,0:T(8,128)(2,1)} %wout_h.1), custom_call_target="tpu_custom_call" | custom-call | tf_op jit(solution)/shard_map/moe_exchange/pallas_call | solution.py:375
  72.1 3.0 %convolution_convert_fusion = bf16[1024,1024]{1,0:T(8,128)(2,1)} fusion(bf16[1024,128]{1,0:T(8,128)(2,1)} %get-tuple-element.7, bf16[128,1024]{1,0:T(8,128)(2,1)} %get-tuple-element.8), kind=kOutput, calls=%fused_computation | convolution fusion | flops 269484032 | bytes 2621440 | tf_op jit(solution)/shard_map/dot_general | solution.py:399

commit v3 on v2

--- a/solution.py
+++ b/solution.py
@@ -30,7 +30,7 @@
     tok, spw, spn, win, wout,
     wsend, wrecv, lw, rnv, dsp, nsend, nrecv, relay_a, relay_b,
     wb, pr, ab, rb, gs, si,
-    hp, hr, hb, ob, po, ab2, ro, so, cb,
+    hp, hr, h_own, hb, ob, po, ab2, ro, so, cb,
     ld_sem, x_send, x_recv, c_send, c_recv, s_send, s_recv, f_send, f_recv,
 ):
     s = lax.axis_index("seq")
@@ -66,6 +66,24 @@
         )
         pl.when(cond)(cp.start)
         pending.append((cond, cp))
+        return cp
+
+    def sent(copies):
+        for cp in copies:
+            for k, (cond, other) in enumerate(pending):
+                if other is cp:
+                    del pending[k]
+                    break
+            if cond is None:
+                cp.wait_send()
+            else:
+                pl.when(cond)(cp.wait_send)
+
+    xn = []
+
+    def piece(d, start, count, k):
+        rows, slot = pl.ds(start, count), d // 2
+        xn.append(remote(nsend.at[d, rows], nrecv.at[slot, rows], x_send.at[k, slot], x_recv.at[k, slot], xdev(d)))
 
     def arrival(dst, send, recv):
         return pltpu.make_async_remote_copy(
@@ -128,6 +146,9 @@
         nsend[d, 0:QT, :] = jnp.dot(t, spn[...], preferred_element_type=F32)
         nsend[d, QT:QT + 8, :] = csn
 
+    sent(list(xw.values()))
+    piece(1, 128, 32, 6)
+    piece(3, 0, 32, 6)
     tot = wsend[0]
     for d in (1, 3, 2):
         xw[d].wait_recv()
@@ -143,15 +164,13 @@
     dsp[x, QT:QT + 16, :] = jnp.broadcast_to(m, (16, 128))
     xd = {d: remote(dsp.at[x], dsp.at[x], x_send.at[1, d], x_recv.at[1, d], xdev(d)) for d in SENDS}
 
+    sent(list(xd.values()))
+    piece(1, 160, 32, 7)
+    piece(3, 32, 32, 7)
     for d in SENDS:
         xd[d].wait_recv()
-    low, high = pl.ds(0, 128), pl.ds(128, QT + 8 - 128)
-    via_a = remote(nsend.at[2, low], relay_a, x_send.at[2, 0], x_recv.at[2, 0], xdev(1))
-    via_b = remote(nsend.at[2, high], relay_b, x_send.at[2, 1], x_recv.at[2, 1], xdev(3))
-    xn = [
-        remote(nsend.at[1, high], nrecv.at[0, high], x_send.at[2, 2], x_recv.at[2, 2], xdev(1)),
-        remote(nsend.at[3, low], nrecv.at[1, low], x_send.at[2, 3], x_recv.at[2, 3], xdev(3)),
-    ]
+    via_a = remote(nsend.at[2, pl.ds(0, 128)], relay_a, x_send.at[2, 0], x_recv.at[2, 0], xdev(1))
+    via_b = remote(nsend.at[2, pl.ds(128, 136)], relay_b, x_send.at[2, 1], x_recv.at[2, 1], xdev(3))
     ms = [dsp[q, QT:QT + 1, :].astype(F32) for q in range(4)]
     mseq = jnp.maximum(jnp.maximum(ms[0], ms[1]), jnp.maximum(ms[2], ms[3]))
     total = jnp.zeros((1, 128), F32)
@@ -184,23 +203,27 @@
     m2 = jnp.maximum(m_a, m_b)
     f_a, f_b = jnp.exp(m_a - m2), jnp.exp(m_b - m2)
     t2 = f_a * wb[c, 0, 33:34, :] + f_b * pr[0, 33:34, :]
-    stats = jnp.concatenate([m2, t2, jnp.zeros((6, 128), F32)], axis=0)
+    t_hi = t2.astype(BF16).astype(F32)
+    stats = jnp.concatenate([m2, t_hi, t2 - t_hi, jnp.zeros((13, 128), F32)], axis=0).astype(BF16)
     c_a, c_b = column(f_a), column(f_b)
     for i in range(CHIPS):
         e = i // 2
         k_a, k_b = c_a[e * 16:(e + 1) * 16], c_b[e * 16:(e + 1) * 16]
         for b in range(2):
             r = slice(b * 16, (b + 1) * 16)
-            ab[i, r, :] = wb[c, i, r, :] * k_a + pr[i, r, :] * k_b
-        ab[i, 32:40, :] = stats
+            ab[i, r, :] = (wb[c, i, r, :] * k_a + pr[i, r, :] * k_b).astype(BF16)
+        ab[i, 32:48, :] = stats
     sw = {
         j: remote(ab.at[chip_of(j)], rb.at[j], s_send.at[0, j], s_recv.at[0, j], (chip_of(j) * 2 + c, x))
         for j in range(1, CHIPS)
     }
     for j in range(1, CHIPS):
         sw[j].wait_recv()
-    mr = [ab[p, 32:33, :]] + [rb[j, 32:33, :] for j in range(1, CHIPS)]
-    tr = [ab[p, 33:34, :]] + [rb[j, 33:34, :] for j in range(1, CHIPS)]
+    piece(1, 192, 72, 8)
+    piece(3, 64, 64, 8)
+    st = [ab[p, 32:48, :].astype(F32)] + [rb[j, 32:48, :].astype(F32) for j in range(1, CHIPS)]
+    mr = [v[0:1] for v in st]
+    tr = [v[1:2] + v[2:3] for v in st]
     top = mr[0]
     for v in mr[1:]:
         top = jnp.maximum(top, v)
@@ -216,7 +239,7 @@
         for b in range(2):
             r = slice(b * 16, (b + 1) * 16)
             v = ab[p, r, :] if j == 0 else rb[j, r, :]
-            acc[b] = acc[b] + v * w
+            acc[b] = acc[b] + v.astype(F32) * w
     si[p, c, :, :] = jnp.concatenate(acc, axis=0).astype(BF16)
 
 
@@ -242,6 +265,7 @@
 
     arrive, whole = gather(si, 1)
 
+    xp = []
     arrive(GROUPS[0])
     for i, dz in enumerate(GROUPS):
         if i < 3:
@@ -250,32 +274,45 @@
         q = lax.rem(z + 4 - dz, 4)
         d = lax.rem(q + 4 - x, 4)
         ld_win[dz].wait()
+        own = []
         for k in range(2):
             e = 2 * q + k
             rows = jnp.concatenate(
                 [si[e * 2 + h, g, b * 16:(b + 1) * 16, :] for h in range(2) for g in range(2) for b in range(2)],
                 axis=1,
             )
-            hp[dz, k * 16:(k + 1) * 16, :] = jnp.dot(rows, win[e], preferred_element_type=F32)
-        remote_if(d != 0, hp.at[dz], hr.at[d], x_send.at[3, dz], x_recv.at[3, d], (s, q))
+            own.append(jnp.dot(rows, win[e], preferred_element_type=F32))
+        own = jnp.concatenate(own, axis=0)
+        hp[dz] = own.astype(BF16)
+        xp.append(remote_if(d != 0, hp.at[dz], hr.at[d], x_send.at[3, dz], x_recv.at[3, d], (s, q)))
 
         @pl.when(d == 0)
-        def _(dz=dz):
-            hr[0] = hp[dz]
+        def _(own=own):
+            h_own[...] = own
 
     xh = {d: arrival(hr.at[d], x_send.at[3, 0], x_recv.at[3, d]) for d in (1, 2, 3)}
-    hidden = hr[0]
+    via_a.wait_recv()
+    nsend[1, 0:128, :] = nsend[1, 0:128, :] + relay_a[...]
+    via_b.wait_recv()
+    nsend[3, 128:264, :] = nsend[3, 128:264, :] + relay_b[...]
+    sent(xp)
+    piece(1, 0, 32, 9)
+    piece(3, 128, 32, 9)
+    hidden = h_own[...]
     for d in (1, 3, 2):
         xh[d].wait_recv()
-        hidden = hidden + hr[d]
+        hidden = hidden + hr[d].astype(F32)
     hidden = 0.5 * hidden * (1.0 + lax.erf(hidden * 0.7071067811865476))
     hb[x] = hidden.astype(BF16)
     xg = {d: remote(hb.at[x], hb.at[x], x_send.at[4, d], x_recv.at[4, d], xdev(d)) for d in SENDS}
 
+    sent(list(xg.values()))
+    piece(1, 32, 96, 10)
+    piece(3, 160, 104, 10)
     def chips_sum(q, copy):
         copy.wait_recv()
         block = pl.ds(4 * q, 4)
-        ab2[block] = ob[c, block] + po[block]
+        ab2[block] = (ob[c, block] + po[block]).astype(BF16)
         dz = lax.rem(q + 4 - z, 4)
         for dy in range(4):
             to = q * 4 + lax.rem(y + dy, 4)
@@ -305,15 +342,16 @@
         if last is not None:
             chips_sum(*last)
         last = (q, copy)
-        if d == 0:
-            via_a.wait_recv()
-            nsend[1, low, :] = nsend[1, low, :] + relay_a[...]
-            xn.append(remote(nsend.at[1, low], nrecv.at[0, low], x_send.at[6, 0], x_recv.at[6, 0], xdev(1)))
-            via_b.wait_recv()
-            nsend[3, high, :] = nsend[3, high, :] + relay_b[...]
-            xn.append(remote(nsend.at[3, high], nrecv.at[1, high], x_send.at[6, 1], x_recv.at[6, 1], xdev(3)))
     chips_sum(*last)
     sv = {j: arrival(ro.at[j], s_send.at[2, 0], s_recv.at[2, j]) for j in range(1, CHIPS)}
+    for j in range(1, CHIPS):
+        sv[j].wait_recv()
+    acc = ab2[p].astype(F32)
+    for j in range(1, CHIPS):
+        acc = acc + ro[j].astype(F32)
+    so[p, c, :, :] = acc.astype(BF16)
+    arrive, whole = gather(so, 3)
+
     for cp in xn:
         cp.wait_recv()
     cs = nsend[0, QT:QT + 8, :] + nrecv[0, QT:QT + 8, :] + nrecv[1, QT:QT + 8, :]
@@ -339,64 +377,86 @@
         cb[x, r, :] = (ew / ttot).astype(BF16)
     xc = {d: remote(cb.at[x], cb.at[x], x_send.at[5, d], x_recv.at[5, d], xdev(d)) for d in SENDS}
 
-    for j in range(1, CHIPS):
-        sv[j].wait_recv()
-    acc = ab2[p]
-    for j in range(1, CHIPS):
-        acc = acc + ro[j]
-    so[p, c, :, :] = acc.astype(BF16)
-    arrive, whole = gather(so, 3)
     for dz in GROUPS:
         arrive(dz)
+    for d in SENDS:
+        xc[d].wait_recv()
+    store_comb = load(cb, comb_o, 14)
     for dz in GROUPS:
         whole(dz)
-    for d in SENDS:
-        xc[d].wait_recv()
-    for q in range(4):
-        comb_o[q * QT:(q + 1) * QT, :] = cb[q]
+    load(so, so_o, 15).wait()
+    store_comb.wait()
+    for cond, cp in pending:
+        if cond is None:
+            cp.wait_send()
+        else:
+            pl.when(cond)(cp.wait_send)
+
+
+def mix(comb_h, so_h, out_h, comb, so, slot_out, out, sem):
+    def copy(src, dst, i):
+        cp = pltpu.make_async_copy(src, dst, sem.at[i])
+        cp.start()
+        return cp
+
+    ld_so = copy(so_h, so, 8)
+    ld_comb = [copy(comb_h.at[g], comb.at[g], 4 + g) for g in range(4)]
+    ld_so.wait()
     for e in range(E_RUN):
         for h in range(2):
             for g in range(2):
                 for b in range(2):
                     at = h * 512 + g * 256 + b * 128
-                    so_o[e * 16:(e + 1) * 16, at:at + 128] = so[e * 2 + h, g, b * 16:(b + 1) * 16, :]
-    for cond, cp in pending:
-        if cond is None:
-            cp.wait_send()
-        else:
-            pl.when(cond)(cp.wait_send)
+                    slot_out[e * 16:(e + 1) * 16, at:at + 128] = so[e * 2 + h, g, b * 16:(b + 1) * 16, :]
+    stores = []
+    for g in range(4):
+        ld_comb[g].wait()
+        r = pl.ds(g * QT, QT)
+        out[r, :] = jnp.dot(comb[g], slot_out[...], preferred_element_type=F32).astype(BF16)
+        stores.append(copy(out.at[r], out_h.at[r], g))
+    for cp in stores:
+        cp.wait()
 
 
 def per_device(tokens, slot_param, scale, w_in, w_out):
     vm = pltpu.VMEM
     dma = pltpu.SemaphoreType.DMA
     anyspec = pl.BlockSpec(memory_space=pl.ANY)
-    vspec = pl.BlockSpec(memory_space=pltpu.VMEM)
     comb, slot_out = pl.pallas_call(
         kernel,
         name="moe_exchange",
-        out_shape=(jax.ShapeDtypeStruct((1024, 128), BF16), jax.ShapeDtypeStruct((128, 1024), BF16)),
+        out_shape=(jax.ShapeDtypeStruct((4, QT, 128), BF16), jax.ShapeDtypeStruct((16, 2, 32, 128), BF16)),
         in_specs=[anyspec, anyspec, pl.BlockSpec(memory_space=pltpu.SMEM), anyspec, anyspec],
-        out_specs=(vspec, vspec),
+        out_specs=(anyspec, anyspec),
         scratch_shapes=[
             vm((1024, 1024), BF16), vm((1024, 128), BF16), vm((1024, REST), BF16),
             vm((8, 1024, 512), BF16), vm((8, 512, 1024), BF16),
             vm((4, QT + 8, 128), F32), vm((4, QT + 8, 128), F32), vm((QT, 128), F32), vm((QT, 128), F32),
             vm((4, QT + 16, 128), BF16),
             vm((4, QT + 8, REST), F32), vm((2, QT + 8, REST), F32), vm((128, REST), F32), vm((QT - 120, REST), F32),
-            vm((2, 16, 40, 128), F32), vm((16, 40, 128), F32), vm((16, 40, 128), F32), vm((16, 40, 128), F32),
+            vm((2, 16, 40, 128), F32), vm((16, 40, 128), F32), vm((16, 48, 128), BF16), vm((16, 48, 128), BF16),
             vm((128, 128), F32), vm((16, 2, 32, 128), BF16),
-            vm((4, 32, 512), F32), vm((4, 32, 512), F32), vm((4, 32, 512), BF16),
-            vm((2, 16, 32, 128), F32), vm((16, 32, 128), F32), vm((16, 32, 128), F32), vm((16, 32, 128), F32),
+            vm((4, 32, 512), BF16), vm((4, 32, 512), BF16), vm((32, 512), F32), vm((4, 32, 512), BF16),
+            vm((2, 16, 32, 128), F32), vm((16, 32, 128), F32), vm((16, 32, 128), BF16), vm((16, 32, 128), BF16),
             vm((16, 2, 32, 128), BF16), vm((4, QT, 128), BF16),
-            dma((14,)), dma((7, 4)), dma((7, 4)), dma((5,)), dma((5,)),
+            dma((16,)), dma((12, 4)), dma((12, 4)), dma((5,)), dma((5,)),
             dma((4, 16)), dma((4, 16)), dma((4, 16)), dma((4, 16)),
         ],
         compiler_params=pltpu.CompilerParams(
-            collective_id=0, has_side_effects=True, vmem_limit_bytes=56 * 2**20
+            collective_id=0, has_side_effects=True, vmem_limit_bytes=53 * 2**20
         ),
     )(tokens, slot_param, scale, w_in, w_out)
-    return jnp.dot(comb, slot_out, preferred_element_type=F32).astype(BF16)
+    return pl.pallas_call(
+        mix,
+        name="mix",
+        out_shape=jax.ShapeDtypeStruct((1024, 1024), BF16),
+        in_specs=[anyspec, anyspec],
+        out_specs=anyspec,
+        scratch_shapes=[
+            vm((4, QT, 128), BF16), vm((16, 2, 32, 128), BF16), vm((128, 1024), BF16), vm((1024, 1024), BF16), dma((9,)),
+        ],
+        compiler_params=pltpu.CompilerParams(vmem_limit_bytes=16 * 2**20),
+    )(comb, slot_out)
 
 
 def solution(mesh):

time: 75.3 us -> 66.7 us (0.89)
  Pallas kernels: 71.5 us -> 66 us
  matrix products: 3.04 us -> 0 us
    pallas_call x1, Pallas kernels: 71.5 us -> 63.5 us  [per_device(): pl.pallas_call(kernel, name='moe_exchange', out_shape=(jax.ShapeDtypeStru...]
    dot_general x1 -> x0, matrix products: 3.04 us -> none  [per_device(): return jnp.dot(comb, slot_out, preferred_element_type=F32).astype(BF16)]
    pallas_call x0 -> x1, Pallas kernels: none -> 2.42 us  [per_device(): pl.pallas_call(mix, name='mix', out_shape=jax.ShapeDtypeStruct((1024, 102...]
where the time goes in v3:
time: 66.7 us; the launch traced here: 66.6 us
  Pallas kernels  66 us (99%)
    pallas_call x1, Pallas kernels, per_device(): pl.pallas_call(kernel, name='moe_exchange', out_shape=(jax.ShapeDtypeStru...  63.5 us
    pallas_call x1, Pallas kernels, per_device(): pl.pallas_call(mix, name='mix', out_shape=jax.ShapeDtypeStruct((1024, 102...  2.42 us

profile of v3, /device:TPU:1, one launch (start us, length us, event | category | flops | bytes accessed | tf_op | source)
XLA Modules:
  0.0 66.6 jit_solution(4465124963264699717)
XLA Ops:
  0.7 63.5 %moe_exchange.1 = (bf16[4,256,128]{2,1,0:T(8,128)(2,1)S(1)}, bf16[16,2,32,128]{3,2,1,0:T(8,128)(2,1)S(1)}) custom-call(bf16[1024,1024]{1,0:T(8,128)(2,1)} %tok_h.1, bf16[1024,1024]{1,0:T(8,128)(2,1)} %sp_h.1, f32[1]{0:T(128)S(6)} %copy.6.scale_ref, bf16[8,1024,512]{2,1,0:T(8,128)(2,1)} %win_h.1, bf16[8,512,1024]{2,1,0:T(8,128)(2,1)} %wout_h.1), custom_call_target="tpu_custom_call" | custom-call | tf_op jit(solution)/shard_map/moe_exchange/pallas_call | solution.py:425
  64.2 2.4 %mix.1 = bf16[1024,1024]{1,0:T(8,128)(2,1)} custom-call(bf16[4,256,128]{2,1,0:T(8,128)(2,1)S(1)} %get-tuple-element.7.comb_h, bf16[16,2,32,128]{3,2,1,0:T(8,128)(2,1)S(1)} %get-tuple-element.8.so_h), custom_call_target="tpu_custom_call" | custom-call | tf_op jit(solution)/shard_map/mix/pallas_call | solution.py:449

commit v4 on v3

--- a/solution.py
+++ b/solution.py
@@ -20,18 +20,26 @@
 GROUPS = (0, 1, 3, 2)
 
 
+def hops(j):
+    return (0, 1, 2, 1)[j // 4] + (0, 1, 2, 1)[j % 4]
+
+
+AXIS = (8, 2, 4, 12, 1, 3)
+OTHERS = sorted(range(1, CHIPS), key=lambda j: -hops(j))
+
+
 def column(row):
     return jnp.transpose(jnp.broadcast_to(row, (128, 128)))
 
 
 def kernel(
-    tok_h, sp_h, scale_ref, win_h, wout_h,
+    tok_h, sp_h, scale_h, win_h, wout_h,
     comb_o, so_o,
-    tok, spw, spn, win, wout,
+    scale_ref, tok, spw, spn, win, wout,
     wsend, wrecv, lw, rnv, dsp, nsend, nrecv, relay_a, relay_b,
     wb, pr, ab, rb, gs, si,
     hp, hr, h_own, hb, ob, po, ab2, ro, so, cb,
-    ld_sem, x_send, x_recv, c_send, c_recv, s_send, s_recv, f_send, f_recv,
+    ready, ld_sem, x_send, x_recv, c_send, c_recv, s_send, s_recv, f_send, f_recv,
 ):
     s = lax.axis_index("seq")
     x = lax.axis_index("width")
@@ -50,7 +58,7 @@
     def chip_from(j):
         return lax.rem(z + 4 - j // 4, 4) * 4 + lax.rem(y + 4 - j % 4, 4)
 
-    pending = []
+    pending, bulk = [], []
 
     def remote(src, dst, send, recv, to):
         cp = pltpu.make_async_remote_copy(
@@ -79,35 +87,45 @@
             else:
                 pl.when(cond)(cp.wait_send)
 
+    def drain(count):
+        for cond, cp in pending[:count]:
+            if cond is None:
+                cp.wait_send()
+            else:
+                pl.when(cond)(cp.wait_send)
+        del pending[:count]
+
     xn = []
 
     def piece(d, start, count, k):
         rows, slot = pl.ds(start, count), d // 2
         xn.append(remote(nsend.at[d, rows], nrecv.at[slot, rows], x_send.at[k, slot], x_recv.at[k, slot], xdev(d)))
+        bulk.append(pending.pop())
 
     def arrival(dst, send, recv):
         return pltpu.make_async_remote_copy(
             src_ref=dst, dst_ref=dst, send_sem=send, recv_sem=recv, device_id=peer, device_id_type=MESH
         )
 
+    barrier = pltpu.get_barrier_semaphore()
+    for j in AXIS:
+        pl.semaphore_signal(barrier, inc=1, device_id=(chip_of(j) * 2 + c, x), device_id_type=MESH)
+    for d in SENDS:
+        pl.semaphore_signal(barrier, inc=1, device_id=xdev(d), device_id_type=MESH)
+    pl.semaphore_signal(barrier, inc=1, device_id=peer, device_id_type=MESH)
+
     def load(src, dst, i):
         cp = pltpu.make_async_copy(src, dst, ld_sem.at[i])
         cp.start()
         return cp
 
+    ld_scale = load(scale_h, scale_ref, 16)
     ld_spw = load(sp_h.at[:, pl.ds(0, WINDOW)], spw, 0)
     ld_tok = {}
     for i, d in enumerate((2, 1, 3, 0)):
         rows = pl.ds(lax.rem(x + d, 4) * QT, QT)
         ld_tok[d] = load(tok_h.at[rows], tok.at[rows], 1 + i)
     ld_spn = load(sp_h.at[:, pl.ds(WINDOW, REST)], spn, 5)
-    barrier = pltpu.get_barrier_semaphore()
-    for d in (1, 2, 3):
-        pl.semaphore_signal(barrier, inc=1, device_id=xdev(d), device_id_type=MESH)
-    pl.semaphore_signal(barrier, inc=1, device_id=peer, device_id_type=MESH)
-    for j in range(1, CHIPS):
-        pl.semaphore_signal(barrier, inc=1, device_id=(chip_of(j) * 2 + c, x), device_id_type=MESH)
-
     ld_spw.wait()
     spf = spw[...].astype(F32)
     csq = jnp.sum(spf * spf, axis=0, keepdims=True)
@@ -123,9 +141,12 @@
         rows = [jnp.sum(jnp.transpose(part[h * 128:(h + 1) * 128]), axis=0, keepdims=True) for h in range(2)]
         wsend[d, QT:QT + 8, :] = jnp.concatenate(rows + [csq, jnp.zeros((5, 128), F32)], axis=0)
         if d == 2:
-            pl.semaphore_wait(barrier, 19)
+            pl.semaphore_wait(barrier, 4 + len(AXIS))
         if d:
             xw[d] = remote(wsend.at[d], wrecv.at[d], x_send.at[0, d], x_recv.at[0, d], xdev(d))
+    for j in (8, 4, 12):
+        pl.semaphore_signal(ready, inc=1, device_id=(chip_of(j) * 2 + c, x), device_id_type=MESH)
+
     ld_win = {}
     for i, dz in enumerate(GROUPS):
         e = 2 * lax.rem(z + 4 - dz, 4)
@@ -155,6 +176,7 @@
         tot = tot + wrecv[d]
     rn = jnp.sqrt(jnp.concatenate([column(tot[QT:QT + 1]), column(tot[QT + 1:QT + 2])], axis=0) + EPS)
     cn = jnp.sqrt(tot[QT + 2:QT + 3] + EPS)
+    ld_scale.wait()
     scale = scale_ref[0]
     logits = scale * tot[0:QT] / (rn * cn)
     lw[...] = logits
@@ -171,6 +193,7 @@
         xd[d].wait_recv()
     via_a = remote(nsend.at[2, pl.ds(0, 128)], relay_a, x_send.at[2, 0], x_recv.at[2, 0], xdev(1))
     via_b = remote(nsend.at[2, pl.ds(128, 136)], relay_b, x_send.at[2, 1], x_recv.at[2, 1], xdev(3))
+    bulk.extend((pending.pop(), pending.pop()))
     ms = [dsp[q, QT:QT + 1, :].astype(F32) for q in range(4)]
     mseq = jnp.maximum(jnp.maximum(ms[0], ms[1]), jnp.maximum(ms[2], ms[3]))
     total = jnp.zeros((1, 128), F32)
@@ -213,10 +236,12 @@
             r = slice(b * 16, (b + 1) * 16)
             ab[i, r, :] = (wb[c, i, r, :] * k_a + pr[i, r, :] * k_b).astype(BF16)
         ab[i, 32:48, :] = stats
+    pl.semaphore_wait(ready, 3)
     sw = {
         j: remote(ab.at[chip_of(j)], rb.at[j], s_send.at[0, j], s_recv.at[0, j], (chip_of(j) * 2 + c, x))
-        for j in range(1, CHIPS)
+        for j in OTHERS
     }
+    drain(len(pending) - 15)
     for j in range(1, CHIPS):
         sw[j].wait_recv()
     piece(1, 192, 72, 8)
@@ -244,26 +269,29 @@
 
 
     def gather(buf, k):
-        fwd = {0: remote(buf.at[p, c], buf.at[p, c], f_send.at[k, 0], f_recv.at[k, 0], peer)}
-        out = {
-            j: remote(buf.at[p, c], buf.at[p, c], s_send.at[k, j], s_recv.at[k, j], (chip_of(j) * 2 + c, x))
-            for j in range(1, CHIPS)
-        }
+        out, other = {}, {}
+        for j in OTHERS:
+            to = (chip_of(j) * 2 + c, x)
+            out[j] = remote(buf.at[p, c], buf.at[p, c], s_send.at[k, j], s_recv.at[k, j], to)
+        other[0] = remote(buf.at[p, c], buf.at[p, c], f_send.at[k, 0], f_recv.at[k, 0], peer)
 
         def arrive(dz):
             for j in range(dz * 4, dz * 4 + 4):
                 if j:
                     out[j].wait_recv()
                     at = chip_from(j)
-                    fwd[j] = remote(buf.at[at, c], buf.at[at, c], f_send.at[k, j], f_recv.at[k, j], peer)
+                    other[j] = remote(buf.at[at, c], buf.at[at, c], f_send.at[k, j], f_recv.at[k, j], peer)
 
         def whole(dz):
             for j in range(dz * 4, dz * 4 + 4):
-                fwd[j].wait_recv()
+                other[j].wait_recv()
 
         return arrive, whole
 
+    count = len(pending)
     arrive, whole = gather(si, 1)
+    drain(count)
+    count = len(pending)
 
     xp = []
     arrive(GROUPS[0])
@@ -290,6 +318,7 @@
         def _(own=own):
             h_own[...] = own
 
+    drain(count)
     xh = {d: arrival(hr.at[d], x_send.at[3, 0], x_recv.at[3, d]) for d in (1, 2, 3)}
     via_a.wait_recv()
     nsend[1, 0:128, :] = nsend[1, 0:128, :] + relay_a[...]
@@ -306,6 +335,7 @@
     hb[x] = hidden.astype(BF16)
     xg = {d: remote(hb.at[x], hb.at[x], x_send.at[4, d], x_recv.at[4, d], xdev(d)) for d in SENDS}
 
+    drain(len(pending) - 3)
     sent(list(xg.values()))
     piece(1, 32, 96, 10)
     piece(3, 160, 104, 10)
@@ -323,6 +353,7 @@
             else:
                 remote_if(dz != 0, *args)
 
+    count = len(pending)
     last = None
     for i, d in enumerate(ARRIVALS):
         q = lax.rem(x + 4 - d, 4)
@@ -343,6 +374,7 @@
             chips_sum(*last)
         last = (q, copy)
     chips_sum(*last)
+    drain(count)
     sv = {j: arrival(ro.at[j], s_send.at[2, 0], s_recv.at[2, j]) for j in range(1, CHIPS)}
     for j in range(1, CHIPS):
         sv[j].wait_recv()
@@ -350,7 +382,9 @@
     for j in range(1, CHIPS):
         acc = acc + ro[j].astype(F32)
     so[p, c, :, :] = acc.astype(BF16)
+    count = len(pending)
     arrive, whole = gather(so, 3)
+    drain(count)
 
     for cp in xn:
         cp.wait_recv()
@@ -386,22 +420,19 @@
         whole(dz)
     load(so, so_o, 15).wait()
     store_comb.wait()
-    for cond, cp in pending:
+    for cond, cp in pending + bulk:
         if cond is None:
             cp.wait_send()
         else:
             pl.when(cond)(cp.wait_send)
 
 
-def mix(comb_h, so_h, out_h, comb, so, slot_out, out, sem):
+def mix(comb, so, out_h, slot_out, out, sem):
     def copy(src, dst, i):
         cp = pltpu.make_async_copy(src, dst, sem.at[i])
         cp.start()
         return cp
 
-    ld_so = copy(so_h, so, 8)
-    ld_comb = [copy(comb_h.at[g], comb.at[g], 4 + g) for g in range(4)]
-    ld_so.wait()
     for e in range(E_RUN):
         for h in range(2):
             for g in range(2):
@@ -410,7 +441,6 @@
                     slot_out[e * 16:(e + 1) * 16, at:at + 128] = so[e * 2 + h, g, b * 16:(b + 1) * 16, :]
     stores = []
     for g in range(4):
-        ld_comb[g].wait()
         r = pl.ds(g * QT, QT)
         out[r, :] = jnp.dot(comb[g], slot_out[...], preferred_element_type=F32).astype(BF16)
         stores.append(copy(out.at[r], out_h.at[r], g))
@@ -426,10 +456,10 @@
         kernel,
         name="moe_exchange",
         out_shape=(jax.ShapeDtypeStruct((4, QT, 128), BF16), jax.ShapeDtypeStruct((16, 2, 32, 128), BF16)),
-        in_specs=[anyspec, anyspec, pl.BlockSpec(memory_space=pltpu.SMEM), anyspec, anyspec],
+        in_specs=[anyspec, anyspec, anyspec, anyspec, anyspec],
         out_specs=(anyspec, anyspec),
         scratch_shapes=[
-            vm((1024, 1024), BF16), vm((1024, 128), BF16), vm((1024, REST), BF16),
+            pltpu.SMEM((1,), F32), vm((1024, 1024), BF16), vm((1024, 128), BF16), vm((1024, REST), BF16),
             vm((8, 1024, 512), BF16), vm((8, 512, 1024), BF16),
             vm((4, QT + 8, 128), F32), vm((4, QT + 8, 128), F32), vm((QT, 128), F32), vm((QT, 128), F32),
             vm((4, QT + 16, 128), BF16),
@@ -439,7 +469,7 @@
             vm((4, 32, 512), BF16), vm((4, 32, 512), BF16), vm((32, 512), F32), vm((4, 32, 512), BF16),
             vm((2, 16, 32, 128), F32), vm((16, 32, 128), F32), vm((16, 32, 128), BF16), vm((16, 32, 128), BF16),
             vm((16, 2, 32, 128), BF16), vm((4, QT, 128), BF16),
-            dma((16,)), dma((12, 4)), dma((12, 4)), dma((5,)), dma((5,)),
+            pltpu.SemaphoreType.REGULAR, dma((17,)), dma((12, 4)), dma((12, 4)), dma((5,)), dma((5,)),
             dma((4, 16)), dma((4, 16)), dma((4, 16)), dma((4, 16)),
         ],
         compiler_params=pltpu.CompilerParams(
@@ -450,11 +480,9 @@
         mix,
         name="mix",
         out_shape=jax.ShapeDtypeStruct((1024, 1024), BF16),
-        in_specs=[anyspec, anyspec],
+        in_specs=[pl.BlockSpec(memory_space=pltpu.VMEM)] * 2,
         out_specs=anyspec,
-        scratch_shapes=[
-            vm((4, QT, 128), BF16), vm((16, 2, 32, 128), BF16), vm((128, 1024), BF16), vm((1024, 1024), BF16), dma((9,)),
-        ],
+        scratch_shapes=[vm((128, 1024), BF16), vm((1024, 1024), BF16), dma((4,))],
         compiler_params=pltpu.CompilerParams(vmem_limit_bytes=16 * 2**20),
     )(comb, slot_out)
 

time: 66.7 us -> 64.1 us (0.961)
  Pallas kernels: 66 us -> 63.3 us
    pallas_call x1, Pallas kernels: 63.5 us -> 61.7 us  [per_device(): pl.pallas_call(kernel, name='moe_exchange', out_shape=(jax.ShapeDtypeStru...]
    pallas_call x1, Pallas kernels: 2.42 us -> 1.66 us  [per_device(): pl.pallas_call(mix, name='mix', out_shape=jax.ShapeDtypeStruct((1024, 102...]
where the time goes in v4:
time: 64.1 us; the launch traced here: 64 us
  Pallas kernels  63.3 us (99%)
  between operations  0.66 us (1%)
    pallas_call x1, Pallas kernels, per_device(): pl.pallas_call(kernel, name='moe_exchange', out_shape=(jax.ShapeDtypeStru...  61.7 us
    pallas_call x1, Pallas kernels, per_device(): pl.pallas_call(mix, name='mix', out_shape=jax.ShapeDtypeStruct((1024, 102...  1.66 us

profile of v4, /device:TPU:1, one launch (start us, length us, event | category | flops | bytes accessed | tf_op | source)
XLA Modules:
  0.0 64.0 jit_solution(15328372401448614833)
XLA Ops:
  0.7 61.7 %moe_exchange.1 = (bf16[4,256,128]{2,1,0:T(8,128)(2,1)S(1)}, bf16[16,2,32,128]{3,2,1,0:T(8,128)(2,1)S(1)}) custom-call(bf16[1024,1024]{1,0:T(8,128)(2,1)} %tok_h.1, bf16[1024,1024]{1,0:T(8,128)(2,1)} %sp_h.1, f32[1]{0:T(128)S(6)} %copy.6.scale_h, bf16[8,1024,512]{2,1,0:T(8,128)(2,1)} %win_h.1, bf16[8,512,1024]{2,1,0:T(8,128)(2,1)} %wout_h.1), custom_call_target="tpu_custom_call" | custom-call | tf_op jit(solution)/shard_map/moe_exchange/pallas_call | solution.py:455
  62.3 1.7 %mix.1 = bf16[1024,1024]{1,0:T(8,128)(2,1)} custom-call(bf16[4,256,128]{2,1,0:T(8,128)(2,1)S(1)} %get-tuple-element.7.comb, bf16[16,2,32,128]{3,2,1,0:T(8,128)(2,1)S(1)} %get-tuple-element.8.so), custom_call_target="tpu_custom_call" | custom-call | tf_op jit(solution)/shard_map/mix/pallas_call | solution.py:479

commit v5 on v4

--- a/solution.py
+++ b/solution.py
@@ -36,9 +36,9 @@
     tok_h, sp_h, scale_h, win_h, wout_h,
     comb_o, so_o,
     scale_ref, tok, spw, spn, win, wout,
-    wsend, wrecv, lw, rnv, dsp, nsend, nrecv, relay_a, relay_b,
+    wsend, wrecv, lw, rnv, dsp, cq, nsend, nrecv, relay_a, relay_b,
     wb, pr, ab, rb, gs, si,
-    hp, hr, h_own, hb, ob, po, ab2, ro, so, cb,
+    hp, hr, h_own, h_half, hb, ob, po, ab2, ro, so, cb,
     ready, ld_sem, x_send, x_recv, c_send, c_recv, s_send, s_recv, f_send, f_recv,
 ):
     s = lax.axis_index("seq")
@@ -162,14 +162,16 @@
         sf = spn[b * 32:(b + 1) * 32, :].astype(F32)
         sq = sf * sf
         csn = csn + sq[0:8] + sq[8:16] + sq[16:24] + sq[24:32]
+    csr = jnp.sum(csn, axis=0, keepdims=True)
+    cq[0] = jnp.concatenate([csr[:, b * 128:(b + 1) * 128] for b in range(7)] + [jnp.ones((1, 128), F32)], axis=0)
+    xq = {d: remote(cq.at[0], cq.at[d], x_send.at[11, d], x_recv.at[11, d], xdev(d)) for d in SENDS}
     for d in (2, 1, 3, 0):
         t = tok[pl.ds(lax.rem(x + d, 4) * QT, QT), :]
         nsend[d, 0:QT, :] = jnp.dot(t, spn[...], preferred_element_type=F32)
-        nsend[d, QT:QT + 8, :] = csn
 
     sent(list(xw.values()))
-    piece(1, 128, 32, 6)
-    piece(3, 0, 32, 6)
+    piece(1, 128, 40, 6)
+    piece(3, 0, 40, 6)
     tot = wsend[0]
     for d in (1, 3, 2):
         xw[d].wait_recv()
@@ -187,12 +189,12 @@
     xd = {d: remote(dsp.at[x], dsp.at[x], x_send.at[1, d], x_recv.at[1, d], xdev(d)) for d in SENDS}
 
     sent(list(xd.values()))
-    piece(1, 160, 32, 7)
-    piece(3, 32, 32, 7)
+    piece(1, 168, 32, 7)
+    piece(3, 40, 32, 7)
     for d in SENDS:
         xd[d].wait_recv()
     via_a = remote(nsend.at[2, pl.ds(0, 128)], relay_a, x_send.at[2, 0], x_recv.at[2, 0], xdev(1))
-    via_b = remote(nsend.at[2, pl.ds(128, 136)], relay_b, x_send.at[2, 1], x_recv.at[2, 1], xdev(3))
+    via_b = remote(nsend.at[2, pl.ds(128, 128)], relay_b, x_send.at[2, 1], x_recv.at[2, 1], xdev(3))
     bulk.extend((pending.pop(), pending.pop()))
     ms = [dsp[q, QT:QT + 1, :].astype(F32) for q in range(4)]
     mseq = jnp.maximum(jnp.maximum(ms[0], ms[1]), jnp.maximum(ms[2], ms[3]))
@@ -244,8 +246,8 @@
     drain(len(pending) - 15)
     for j in range(1, CHIPS):
         sw[j].wait_recv()
-    piece(1, 192, 72, 8)
-    piece(3, 64, 64, 8)
+    piece(1, 200, 40, 8)
+    piece(3, 72, 40, 8)
     st = [ab[p, 32:48, :].astype(F32)] + [rb[j, 32:48, :].astype(F32) for j in range(1, CHIPS)]
     mr = [v[0:1] for v in st]
     tr = [v[1:2] + v[2:3] for v in st]
@@ -293,24 +295,28 @@
     drain(count)
     count = len(pending)
 
+    def half(dz, g):
+        parts = []
+        for k in range(2):
+            e = 2 * lax.rem(z + 4 - dz, 4) + k
+            part = jnp.zeros((16, 512), F32)
+            for h in range(2):
+                rows = jnp.concatenate([si[e * 2 + h, g, 0:16, :], si[e * 2 + h, g, 16:32, :]], axis=1)
+                at = pl.multiple_of(h * 512 + g * 256, 256)
+                part = part + jnp.dot(rows, win[e, pl.ds(at, 256), :], preferred_element_type=F32)
+            parts.append(part)
+        return jnp.concatenate(parts, axis=0)
+
     xp = []
-    arrive(GROUPS[0])
-    for i, dz in enumerate(GROUPS):
-        if i < 3:
-            arrive(GROUPS[i + 1])
+    for dz in GROUPS:
+        arrive(dz)
+        ld_win[dz].wait()
+        h_half[dz] = half(dz, c)
+    for dz in GROUPS:
         whole(dz)
         q = lax.rem(z + 4 - dz, 4)
         d = lax.rem(q + 4 - x, 4)
-        ld_win[dz].wait()
-        own = []
-        for k in range(2):
-            e = 2 * q + k
-            rows = jnp.concatenate(
-                [si[e * 2 + h, g, b * 16:(b + 1) * 16, :] for h in range(2) for g in range(2) for b in range(2)],
-                axis=1,
-            )
-            own.append(jnp.dot(rows, win[e], preferred_element_type=F32))
-        own = jnp.concatenate(own, axis=0)
+        own = h_half[dz] + half(dz, 1 - c)
         hp[dz] = own.astype(BF16)
         xp.append(remote_if(d != 0, hp.at[dz], hr.at[d], x_send.at[3, dz], x_recv.at[3, d], (s, q)))
 
@@ -323,7 +329,7 @@
     via_a.wait_recv()
     nsend[1, 0:128, :] = nsend[1, 0:128, :] + relay_a[...]
     via_b.wait_recv()
-    nsend[3, 128:264, :] = nsend[3, 128:264, :] + relay_b[...]
+    nsend[3, 128:256, :] = nsend[3, 128:256, :] + relay_b[...]
     sent(xp)
     piece(1, 0, 32, 9)
     piece(3, 128, 32, 9)
@@ -338,7 +344,9 @@
     drain(len(pending) - 3)
     sent(list(xg.values()))
     piece(1, 32, 96, 10)
-    piece(3, 160, 104, 10)
+    piece(3, 160, 96, 10)
+    piece(1, 240, 16, 12)
+    piece(3, 112, 16, 12)
     def chips_sum(q, copy):
         copy.wait_recv()
         block = pl.ds(4 * q, 4)
@@ -388,8 +396,9 @@
 
     for cp in xn:
         cp.wait_recv()
-    cs = nsend[0, QT:QT + 8, :] + nrecv[0, QT:QT + 8, :] + nrecv[1, QT:QT + 8, :]
-    cnn = jnp.sqrt(jnp.sum(cs, axis=0, keepdims=True) + EPS)
+    for d in SENDS:
+        xq[d].wait_recv()
+    cnn = jnp.sqrt(cq[0] + cq[1] + cq[2] + cq[3] + EPS)
     for g in range(4):
         r = slice(g * 64, (g + 1) * 64)
         rg = rnv[r, :]
@@ -399,7 +408,7 @@
         for b in range(7):
             at = slice(b * 128, (b + 1) * 128)
             raw = nsend[0, r, at] + nrecv[0, r, at] + nrecv[1, r, at]
-            lg = scale * raw / (rg * cnn[:, at])
+            lg = scale * raw / (rg * cnn[b:b + 1])
             ls.append(lg)
             top = jnp.maximum(top, lg)
         tmax = jnp.max(top, axis=1, keepdims=True)
@@ -463,13 +472,13 @@
             vm((8, 1024, 512), BF16), vm((8, 512, 1024), BF16),
             vm((4, QT + 8, 128), F32), vm((4, QT + 8, 128), F32), vm((QT, 128), F32), vm((QT, 128), F32),
             vm((4, QT + 16, 128), BF16),
-            vm((4, QT + 8, REST), F32), vm((2, QT + 8, REST), F32), vm((128, REST), F32), vm((QT - 120, REST), F32),
+            vm((4, 8, 128), F32), vm((4, QT, REST), F32), vm((2, QT, REST), F32), vm((128, REST), F32), vm((128, REST), F32),
             vm((2, 16, 40, 128), F32), vm((16, 40, 128), F32), vm((16, 48, 128), BF16), vm((16, 48, 128), BF16),
             vm((128, 128), F32), vm((16, 2, 32, 128), BF16),
-            vm((4, 32, 512), BF16), vm((4, 32, 512), BF16), vm((32, 512), F32), vm((4, 32, 512), BF16),
+            vm((4, 32, 512), BF16), vm((4, 32, 512), BF16), vm((32, 512), F32), vm((4, 32, 512), F32), vm((4, 32, 512), BF16),
             vm((2, 16, 32, 128), F32), vm((16, 32, 128), F32), vm((16, 32, 128), BF16), vm((16, 32, 128), BF16),
             vm((16, 2, 32, 128), BF16), vm((4, QT, 128), BF16),
-            pltpu.SemaphoreType.REGULAR, dma((17,)), dma((12, 4)), dma((12, 4)), dma((5,)), dma((5,)),
+            pltpu.SemaphoreType.REGULAR, dma((17,)), dma((13, 4)), dma((13, 4)), dma((5,)), dma((5,)),
             dma((4, 16)), dma((4, 16)), dma((4, 16)), dma((4, 16)),
         ],
         compiler_params=pltpu.CompilerParams(

time: 64.1 us -> 62.4 us (0.973)
  Pallas kernels: 63.3 us -> 61.6 us
    pallas_call x1, Pallas kernels: 61.7 us -> 59.9 us  [per_device(): pl.pallas_call(kernel, name='moe_exchange', out_shape=(jax.ShapeDtypeStru...]
where the time goes in v5:
time: 62.4 us; the launch traced here: 62.3 us
  Pallas kernels  61.6 us (99%)
  between operations  0.66 us (1%)
    pallas_call x1, Pallas kernels, per_device(): pl.pallas_call(kernel, name='moe_exchange', out_shape=(jax.ShapeDtypeStru...  59.9 us
    pallas_call x1, Pallas kernels, per_device(): pl.pallas_call(mix, name='mix', out_shape=jax.ShapeDtypeStruct((1024, 102...  1.65 us

profile of v5, /device:TPU:1, one launch (start us, length us, event | category | flops | bytes accessed | tf_op | source)
XLA Modules:
  0.0 62.3 jit_solution(15233330955698750195)
XLA Ops:
  0.7 59.9 %moe_exchange.1 = (bf16[4,256,128]{2,1,0:T(8,128)(2,1)S(1)}, bf16[16,2,32,128]{3,2,1,0:T(8,128)(2,1)S(1)}) custom-call(bf16[1024,1024]{1,0:T(8,128)(2,1)} %tok_h.1, bf16[1024,1024]{1,0:T(8,128)(2,1)} %sp_h.1, f32[1]{0:T(128)S(6)} %copy.6.scale_h, bf16[8,1024,512]{2,1,0:T(8,128)(2,1)} %win_h.1, bf16[8,512,1024]{2,1,0:T(8,128)(2,1)} %wout_h.1), custom_call_target="tpu_custom_call" | custom-call | tf_op jit(solution)/shard_map/moe_exchange/pallas_call | solution.py:464
  60.6 1.7 %mix.1 = bf16[1024,1024]{1,0:T(8,128)(2,1)} custom-call(bf16[4,256,128]{2,1,0:T(8,128)(2,1)S(1)} %get-tuple-element.7.comb, bf16[16,2,32,128]{3,2,1,0:T(8,128)(2,1)S(1)} %get-tuple-element.8.so), custom_call_target="tpu_custom_call" | custom-call | tf_op jit(solution)/shard_map/mix/pallas_call | solution.py:488

commit v6 on v5

--- a/solution.py
+++ b/solution.py
@@ -37,7 +37,7 @@
     comb_o, so_o,
     scale_ref, tok, spw, spn, win, wout,
     wsend, wrecv, lw, rnv, dsp, cq, nsend, nrecv, relay_a, relay_b,
-    wb, pr, ab, rb, gs, si,
+    wb, fs, pr, ab, rb, gs, si,
     hp, hr, h_own, h_half, hb, ob, po, ab2, ro, so, cb,
     ready, ld_sem, x_send, x_recv, c_send, c_recv, s_send, s_recv, f_send, f_recv,
 ):
@@ -230,19 +230,19 @@
     t2 = f_a * wb[c, 0, 33:34, :] + f_b * pr[0, 33:34, :]
     t_hi = t2.astype(BF16).astype(F32)
     stats = jnp.concatenate([m2, t_hi, t2 - t_hi, jnp.zeros((13, 128), F32)], axis=0).astype(BF16)
-    c_a, c_b = column(f_a), column(f_b)
-    for i in range(CHIPS):
-        e = i // 2
-        k_a, k_b = c_a[e * 16:(e + 1) * 16], c_b[e * 16:(e + 1) * 16]
+    fs[0], fs[1] = column(f_a), column(f_b)
+    pl.semaphore_wait(ready, 3)
+    sw = {}
+    for j in OTHERS + [0]:
+        i = chip_of(j)
+        rows = pl.ds(lax.div(i, 2) * 16, 16)
+        k_a, k_b = fs[0, rows, :], fs[1, rows, :]
         for b in range(2):
             r = slice(b * 16, (b + 1) * 16)
             ab[i, r, :] = (wb[c, i, r, :] * k_a + pr[i, r, :] * k_b).astype(BF16)
         ab[i, 32:48, :] = stats
-    pl.semaphore_wait(ready, 3)
-    sw = {
-        j: remote(ab.at[chip_of(j)], rb.at[j], s_send.at[0, j], s_recv.at[0, j], (chip_of(j) * 2 + c, x))
-        for j in OTHERS
-    }
+        if j:
+            sw[j] = remote(ab.at[i], rb.at[j], s_send.at[0, j], s_recv.at[0, j], (i * 2 + c, x))
     drain(len(pending) - 15)
     for j in range(1, CHIPS):
         sw[j].wait_recv()
@@ -331,8 +331,8 @@
     via_b.wait_recv()
     nsend[3, 128:256, :] = nsend[3, 128:256, :] + relay_b[...]
     sent(xp)
-    piece(1, 0, 32, 9)
-    piece(3, 128, 32, 9)
+    piece(1, 0, 24, 9)
+    piece(3, 128, 24, 9)
     hidden = h_own[...]
     for d in (1, 3, 2):
         xh[d].wait_recv()
@@ -343,8 +343,8 @@
 
     drain(len(pending) - 3)
     sent(list(xg.values()))
-    piece(1, 32, 96, 10)
-    piece(3, 160, 96, 10)
+    piece(1, 24, 104, 10)
+    piece(3, 152, 104, 10)
     piece(1, 240, 16, 12)
     piece(3, 112, 16, 12)
     def chips_sum(q, copy):
@@ -473,7 +473,7 @@
             vm((4, QT + 8, 128), F32), vm((4, QT + 8, 128), F32), vm((QT, 128), F32), vm((QT, 128), F32),
             vm((4, QT + 16, 128), BF16),
             vm((4, 8, 128), F32), vm((4, QT, REST), F32), vm((2, QT, REST), F32), vm((128, REST), F32), vm((128, REST), F32),
-            vm((2, 16, 40, 128), F32), vm((16, 40, 128), F32), vm((16, 48, 128), BF16), vm((16, 48, 128), BF16),
+            vm((2, 16, 40, 128), F32), vm((2, 128, 128), F32), vm((16, 40, 128), F32), vm((16, 48, 128), BF16), vm((16, 48, 128), BF16),
             vm((128, 128), F32), vm((16, 2, 32, 128), BF16),
             vm((4, 32, 512), BF16), vm((4, 32, 512), BF16), vm((32, 512), F32), vm((4, 32, 512), F32), vm((4, 32, 512), BF16),
             vm((2, 16, 32, 128), F32), vm((16, 32, 128), F32), vm((16, 32, 128), BF16), vm((16, 32, 128), BF16),

time: 62.4 us -> 62.1 us (level)
  no operation moved by 1% of the time
where the time goes in v6:
time: 62.1 us; the launch traced here: 62 us
  Pallas kernels  61.3 us (99%)
  between operations  0.66 us (1%)
    pallas_call x1, Pallas kernels, per_device(): pl.pallas_call(kernel, name='moe_exchange', out_shape=(jax.ShapeDtypeStru...  59.7 us
    pallas_call x1, Pallas kernels, per_device(): pl.pallas_call(mix, name='mix', out_shape=jax.ShapeDtypeStruct((1024, 102...  1.65 us

profile of v6, /device:TPU:1, one launch (start us, length us, event | category | flops | bytes accessed | tf_op | source)
XLA Modules:
  0.0 62.0 jit_solution(9191313658925034548)
XLA Ops:
  0.7 59.7 %moe_exchange.1 = (bf16[4,256,128]{2,1,0:T(8,128)(2,1)S(1)}, bf16[16,2,32,128]{3,2,1,0:T(8,128)(2,1)S(1)}) custom-call(bf16[1024,1024]{1,0:T(8,128)(2,1)} %tok_h.1, bf16[1024,1024]{1,0:T(8,128)(2,1)} %sp_h.1, f32[1]{0:T(128)S(6)} %copy.6.scale_h, bf16[8,1024,512]{2,1,0:T(8,128)(2,1)} %win_h.1, bf16[8,512,1024]{2,1,0:T(8,128)(2,1)} %wout_h.1), custom_call_target="tpu_custom_call" | custom-call | tf_op jit(solution)/shard_map/moe_exchange/pallas_call | solution.py:464
  60.3 1.7 %mix.1 = bf16[1024,1024]{1,0:T(8,128)(2,1)} custom-call(bf16[4,256,128]{2,1,0:T(8,128)(2,1)S(1)} %get-tuple-element.7.comb, bf16[16,2,32,128]{3,2,1,0:T(8,128)(2,1)S(1)} %get-tuple-element.8.so), custom_call_target="tpu_custom_call" | custom-call | tf_op jit(solution)/shard_map/mix/pallas_call | solution.py:488

commit v7 on v6

--- a/solution.py
+++ b/solution.py
@@ -189,8 +189,8 @@
     xd = {d: remote(dsp.at[x], dsp.at[x], x_send.at[1, d], x_recv.at[1, d], xdev(d)) for d in SENDS}
 
     sent(list(xd.values()))
-    piece(1, 168, 32, 7)
-    piece(3, 40, 32, 7)
+    piece(1, 168, 40, 7)
+    piece(3, 40, 40, 7)
     for d in SENDS:
         xd[d].wait_recv()
     via_a = remote(nsend.at[2, pl.ds(0, 128)], relay_a, x_send.at[2, 0], x_recv.at[2, 0], xdev(1))
@@ -246,8 +246,8 @@
     drain(len(pending) - 15)
     for j in range(1, CHIPS):
         sw[j].wait_recv()
-    piece(1, 200, 40, 8)
-    piece(3, 72, 40, 8)
+    piece(1, 208, 32, 8)
+    piece(3, 80, 32, 8)
     st = [ab[p, 32:48, :].astype(F32)] + [rb[j, 32:48, :].astype(F32) for j in range(1, CHIPS)]
     mr = [v[0:1] for v in st]
     tr = [v[1:2] + v[2:3] for v in st]
@@ -449,9 +449,9 @@
                     at = h * 512 + g * 256 + b * 128
                     slot_out[e * 16:(e + 1) * 16, at:at + 128] = so[e * 2 + h, g, b * 16:(b + 1) * 16, :]
     stores = []
-    for g in range(4):
-        r = pl.ds(g * QT, QT)
-        out[r, :] = jnp.dot(comb[g], slot_out[...], preferred_element_type=F32).astype(BF16)
+    for g in range(8):
+        r = pl.ds(g * 128, 128)
+        out[r, :] = jnp.dot(comb[g // 2, g % 2 * 128:g % 2 * 128 + 128, :], slot_out[...], preferred_element_type=F32).astype(BF16)
         stores.append(copy(out.at[r], out_h.at[r], g))
     for cp in stores:
         cp.wait()
@@ -491,7 +491,7 @@
         out_shape=jax.ShapeDtypeStruct((1024, 1024), BF16),
         in_specs=[pl.BlockSpec(memory_space=pltpu.VMEM)] * 2,
         out_specs=anyspec,
-        scratch_shapes=[vm((128, 1024), BF16), vm((1024, 1024), BF16), dma((4,))],
+        scratch_shapes=[vm((128, 1024), BF16), vm((1024, 1024), BF16), dma((8,))],
         compiler_params=pltpu.CompilerParams(vmem_limit_bytes=16 * 2**20),
     )(comb, slot_out)
 

time: 62.1 us -> 62.1 us (level)
  no operation moved by 1% of the time
where the time goes in v7:
time: 62.1 us; the launch traced here: 62 us
  Pallas kernels  61.3 us (99%)
  between operations  0.66 us (1%)
    pallas_call x1, Pallas kernels, per_device(): pl.pallas_call(kernel, name='moe_exchange', out_shape=(jax.ShapeDtypeStru...  59.7 us
    pallas_call x1, Pallas kernels, per_device(): pl.pallas_call(mix, name='mix', out_shape=jax.ShapeDtypeStruct((1024, 102...  1.63 us

profile of v7, /device:TPU:1, one launch (start us, length us, event | category | flops | bytes accessed | tf_op | source)
XLA Modules:
  0.0 62.0 jit_solution(17673956214669385999)
XLA Ops:
  0.7 59.7 %moe_exchange.1 = (bf16[4,256,128]{2,1,0:T(8,128)(2,1)S(1)}, bf16[16,2,32,128]{3,2,1,0:T(8,128)(2,1)S(1)}) custom-call(bf16[1024,1024]{1,0:T(8,128)(2,1)} %tok_h.1, bf16[1024,1024]{1,0:T(8,128)(2,1)} %sp_h.1, f32[1]{0:T(128)S(6)} %copy.6.scale_h, bf16[8,1024,512]{2,1,0:T(8,128)(2,1)} %win_h.1, bf16[8,512,1024]{2,1,0:T(8,128)(2,1)} %wout_h.1), custom_call_target="tpu_custom_call" | custom-call | tf_op jit(solution)/shard_map/moe_exchange/pallas_call | solution.py:464
  60.3 1.6 %mix.1 = bf16[1024,1024]{1,0:T(8,128)(2,1)} custom-call(bf16[4,256,128]{2,1,0:T(8,128)(2,1)S(1)} %get-tuple-element.7.comb, bf16[16,2,32,128]{3,2,1,0:T(8,128)(2,1)S(1)} %get-tuple-element.8.so), custom_call_target="tpu_custom_call" | custom-call | tf_op jit(solution)/shard_map/mix/pallas_call | solution.py:488
